TPU v7x, 256 devices: a whole 4x4x8 slice. The times are simulated.
256 devices in a mesh: pages: 128 (over y_lo, x, z, core), tok: 2 (over y_hi).
Axes of the slice: x: 4, y: 4 (y_hi: 2, y_lo: 2; y = y_hi * 2 + y_lo), z: 8, core: 2. Of those that a mesh axis runs over, the one named last changes fastest.
Arguments:
- queries: bfloat16 [256, 32, 128], P('pages'), may hold values from -50 to 50
- pages: bfloat16 [128, 1024, 128], P('pages', 'tok'), may hold values from -10 to 10
- pad_counts: int32 [128], P('pages'), may hold values from 0 to 511
- labels: int32 [256, 128], P(None, 'pages'), may hold values 0 or 1
Outputs:
- query_grad: float32 [256, 32, 128], P('pages')
- page_grad: float32 [128, 1024, 128], P('pages', 'tok')
- page_loss: float32 [128], P('pages')
All inputs are finite; a program needn't handle non-finite values. No bound on the sum of `labels` on one device may be relied on, other than what follows from the above.
Results may differ from a plain program's by a relative error of at most 0.0025.
Values may be sent and summed in bfloat16 or wider, within the bound.
A program may use at most 64 MiB of HBM per device.

v0:
```python
import math

import jax
import jax.numpy as jnp
from jax import lax
from jax.sharding import Mesh
from jax.sharding import PartitionSpec as P

LP = 1024
PAGES = ("pages_0", "pages_1", "pages_2", "pages_3")


MASKED = -1000000000.0
LOGIT_SPAN = 8.0
CENTRE_SHIFT = 0.5
FILL_SHARE = 0.75


def from_everyone(value, axis):
    length = lax.axis_size(axis)
    return lax.all_to_all(
        jnp.broadcast_to(value[None], (length, *value.shape)), axis, 0, 0, tiled=True
    )


def laid_out(tiles, dim):
    dims = list(tiles.shape[1:])
    dims[dim] *= tiles.shape[0]
    return jnp.moveaxis(tiles, 0, dim).reshape(dims)


def whole_of(value, axes, dim):
    far, near = axes
    first = from_everyone(value, far)
    tiles = jnp.swapaxes(from_everyone(first, near), 0, 1)
    return laid_out(tiles.reshape(-1, *value.shape), dim)


def folded_in_pairs(pieces, combine):
    while len(jax.tree.leaves(pieces)[0]) > 1:
        pieces = jax.vmap(combine)(*(pieces[side::2] for side in (0, 1)))
    return pieces[0]


def combined_all(value, axis, combine):
    pieces = from_everyone(value, axis)
    return folded_in_pairs(pieces, combine)


def split_up(value, dim, length):
    dims = value.shape
    tiles = value.reshape(*dims[:dim], length, dims[dim] // length, *dims[dim + 1 :])
    return jnp.moveaxis(tiles, dim, 0)


def sent_and_summed(value, axis, dim):
    length = lax.axis_size(axis)
    tiles = lax.all_to_all(split_up(value, dim, length), axis, 0, 0, tiled=True)
    return jnp.sum(tiles, axis=0)


def sum_in_two_steps(value, axes, dim):
    far, near = axes
    tiles = split_up(value, dim, lax.axis_size(far))
    nearer = sent_and_summed(tiles, near, dim + 1)
    arrived = lax.all_to_all(nearer, far, split_axis=0, concat_axis=0, tiled=True)
    return arrived.sum(axis=0)


def of_everyone(value, axis):
    everything = from_everyone(value, axis)
    return jnp.sum(everything, axis=0)


def combine_smooth(former, latter):
    highest = jnp.maximum(former, latter)
    return highest + jnp.log(jnp.exp(former - highest) + jnp.exp(latter - highest))


def on_device(queries, pages, pad_counts, labels):
    query_count, query_len, feature_width = queries.shape
    local_pages, local_tokens, _ = pages.shape
    score_scale = feature_width ** (-0.5)
    token_offset = lax.axis_index("tok") * local_tokens
    positions = token_offset + jnp.arange(local_tokens, dtype=jnp.int32)
    usable = positions[None, :] < (LP - pad_counts)[:, None]
    gathered = whole_of(queries, (("pages_0", "pages_1", "pages_2"), "pages_3"), 0)
    query_total = gathered.shape[0]
    row_count = query_total * query_len
    query_rows = gathered.reshape(row_count, feature_width)
    block_rows = math.gcd(row_count, 512)
    block_count = row_count // block_rows

    def scores_for(query_block, page_no):
        raw = (
            lax.dot_general(
                query_block,
                pages[page_no],
                (((1,), (1,)), ((), ())),
                preferred_element_type=jnp.float32,
            )
            * score_scale
        )
        return jnp.where(usable[page_no][None, :], raw, MASKED)

    def forward_block(block_index, running):
        offset = block_index * block_rows
        query_block = lax.dynamic_slice_in_dim(query_rows, offset, block_rows, 0)
        scores = scores_for(query_block, 0)
        highest = jnp.max(scores, axis=1)
        columns = [highest + jnp.log(jnp.sum(jnp.exp(scores - highest[:, None]), axis=1))]
        partial_value = jnp.stack(columns, axis=1)
        return lax.dynamic_update_slice_in_dim(running, partial_value, offset, 0)

    buffered = lax.fori_loop(
        0, block_count, forward_block, jnp.zeros((row_count, local_pages), jnp.float32)
    )
    smooth = combined_all(buffered, "tok", combine_smooth)
    similarity = smooth.reshape(query_total, query_len, local_pages).sum(axis=1)
    label_sign = 2.0 * labels.astype(jnp.float32) - 1.0
    logit_gain = LOGIT_SPAN / query_len
    centre = query_len * (CENTRE_SHIFT + math.log(FILL_SHARE * LP))
    logits = logit_gain * (similarity - centre)
    page_loss = jnp.sum(jax.nn.softplus(-label_sign * logits), axis=0)
    slope = logit_gain * (-label_sign * jax.nn.sigmoid(-label_sign * logits))
    row_slope = jnp.repeat(slope, query_len, axis=0)

    def backward_block(block_index, running):
        query_terms, page_terms = running
        offset = block_index * block_rows
        query_block = lax.dynamic_slice_in_dim(query_rows, offset, block_rows, 0)
        smooth_block = lax.dynamic_slice_in_dim(smooth, offset, block_rows, 0)
        slope_block = lax.dynamic_slice_in_dim(row_slope, offset, block_rows, 0)
        scores = scores_for(query_block, 0)
        weights = jnp.where(usable[0][None, :], jnp.exp(scores - smooth_block[:, 0][:, None]), 0.0)
        scaled = (weights * slope_block[:, 0][:, None]).astype(jnp.bfloat16)
        summed = jnp.dot(scaled, pages[0], preferred_element_type=jnp.float32)
        gradients = [
            lax.dot_general(
                scaled, query_block, (((0,), (0,)), ((), ())), preferred_element_type=jnp.float32
            )
        ]
        page_terms = page_terms + jnp.stack(gradients, axis=0)
        query_terms = lax.dynamic_update_slice_in_dim(query_terms, summed * score_scale, offset, 0)
        return (query_terms, page_terms)

    start_terms = (
        jnp.zeros((row_count, feature_width), jnp.float32),
        jnp.zeros((local_pages, local_tokens, feature_width), jnp.float32),
    )
    query_terms, page_terms = lax.fori_loop(0, block_count, backward_block, start_terms)
    page_grad = page_terms * score_scale
    owned = sum_in_two_steps(query_terms, (("pages_0", "pages_1", "pages_2"), "pages_3"), 0)
    owned = of_everyone(owned, "tok")
    query_grad = owned.reshape(query_count, query_len, feature_width)
    return (query_grad, page_grad, page_loss)


def solution(mesh):
    finer = Mesh(
        mesh.devices.reshape(2, 4, 8, 2, mesh.shape["tok"]),
        ("pages_0", "pages_1", "pages_2", "pages_3", "tok"),
    )
    return jax.shard_map(
        on_device,
        mesh=finer,
        in_specs=(P(PAGES, None, None), P(PAGES, "tok", None), P(PAGES), P(None, PAGES)),
        out_specs=(P(PAGES, None, None), P(PAGES, "tok", None), P(PAGES)),
        check_vma=False,
    )
```

profile of v0, /device:TPU:8, one launch (start us, length us, event | category | flops | bytes accessed | tf_op | source)
XLA Modules:
  0.0 188.4 jit_solution(2626723581054801725)
XLA Ops:
  0.6 2.0 %broadcast_in_dim.109 = bf16[64,2,32,128]{3,2,1,0:T(8,128)(2,1)} broadcast(bf16[2,32,128]{2,1,0:T(8,128)(2,1)} %param.8), dimensions={1,2,3} | broadcast | bytes 1064960 | tf_op jit(solution)/shard_map/broadcast_in_dim | solution.py:22
  2.6 13.0 %all-to-all-start = ((bf16[64,2,32,128]{3,2,1,0:T(8,128)(2,1)}), bf16[64,2,32,128]{3,2,1,0:T(8,128)(2,1)S(1)}, u32[]{:S(2)}, u32[]{:S(2)}) async-start(bf16[64,2,32,128]{3,2,1,0:T(8,128)(2,1)} %broadcast_in_dim.109), calls=%async_computation | async-start | bytes 2097152 | tf_op jit(solution)/shard_map/all_to_all | solution.py:21
  16.3 28.9 %all-to-all-done = bf16[64,2,32,128]{3,2,1,0:T(8,128)(2,1)S(1)} async-done(((bf16[64,2,32,128]{3,2,1,0:T(8,128)(2,1)}), bf16[64,2,32,128]{3,2,1,0:T(8,128)(2,1)S(1)}, u32[]{:S(2)}, u32[]{:S(2)}) %all-to-all-start) | async-done | bytes 1048608 | tf_op jit(solution)/shard_map/all_to_all | solution.py:21
  45.2 0.5 broadcast_in_dim.110
  45.7 5.4 %all_to_all.30 = bf16[2,64,2,32,128]{4,3,2,1,0:T(8,128)(2,1)S(1)} all-to-all(bf16[2,64,2,32,128]{4,3,2,1,0:T(8,128)(2,1)S(1)} %broadcast_in_dim.110), channel_id=1, replica_groups=mesh['pages_0'=2,'pages_1'=4,'pages_2'=8,'pages_3'=2,'tok'=2] {'pages_3'}, dimensions={0} | all-to-all | bytes 4194304 | tf_op jit(solution)/shard_map/all_to_all | solution.py:21
  51.2 0.5 copy.9
  51.6 0.4 copy-done
  52.1 9.5 %while.30 = (s32[]{:T(128)}, f32[8192,1]{0,1:T(1,128)S(1)}, bf16[8192,128]{1,0:T(8,128)(2,1)S(1)}, bf16[1,512,128]{2,1,0:T(8,128)(2,1)S(1)}, s32[]{:T(128)}, /*i...) while((s32[]{:T(128)}, f32[8192,1]{0,1:T(1,128)S(1)}, ...), condition=%wide.region_3.4_spmd.clone, body=%wide.region_0.3_spmd.clone.sunk | while | flops 68420104 | bytes 2376867 | solution.py:115
  61.5 0.7 broadcast_in_dim.113
  62.2 3.6 %all-to-all-start.2 = ((f32[2,8192,1]{1,2,0:T(1,128)}), f32[2,8192,1]{1,2,0:T(1,128)S(1)}, u32[]{:S(2)}, u32[]{:S(2)}) async-start(f32[2,8192,1]{1,2,0:T(1,128)} %broadcast_in_dim.113), calls=%async_computation.2 | async-start | bytes 131072 | tf_op jit(solution)/shard_map/all_to_all | solution.py:21
  65.8 5.6 %all-to-all-done.2 = f32[2,8192,1]{1,2,0:T(1,128)S(1)} async-done(((f32[2,8192,1]{1,2,0:T(1,128)}), f32[2,8192,1]{1,2,0:T(1,128)S(1)}, u32[]{:S(2)}, u32[]{:S(2)}) %all-to-all-start.2) | async-done | bytes 65568 | tf_op jit(solution)/shard_map/all_to_all | solution.py:21
  71.4 0.5 broadcast.110
  71.9 0.8 fusion.25
  73.0 0.6 fusion.23
  73.8 2.2 %broadcast_in_dim.107 = f32[8192,128]{1,0:T(8,128)} broadcast(f32[]{:T(128)} %constant.119.clone.1), dimensions={} | broadcast | bytes 4194308 | tf_op jit(solution)/shard_map/broadcast_in_dim | solution.py:148
  76.0 30.1 %while.31 = (s32[]{:T(128)}, f32[8192,128]{1,0:T(8,128)}, f32[1,512,128]{2,1,0:T(8,128)S(1)}, bf16[8192,128]{1,0:T(8,128)(2,1)S(1)}, bf16[1,512,128]{2,1,0:T(8,1...) while((s32[]{:T(128)}, f32[8192,128]{1,0:T(8,128)}, ...), condition=%wide.region_6.7_spmd.clone, body=%wide.region_5.6_spmd.clone.sunk | while | flops 203097088 | bytes 2897109 | solution.py:151
  76.0 0.4 fusion.46
  76.5 0.4 fusion.48
  76.9 1.0 fusion.47
  77.9 0.4 fusion.46
  78.7 1.0 fusion.47
  79.8 0.4 fusion.46
  80.2 0.4 fusion.48
  80.6 1.0 fusion.47
  81.7 0.4 fusion.46
  82.5 1.0 fusion.47
  83.5 0.4 fusion.46
  84.0 0.4 fusion.48
  84.4 1.0 fusion.47
  85.4 0.4 fusion.46
  85.9 0.4 fusion.48
  86.3 1.0 fusion.47
  87.3 0.4 fusion.46
  88.1 1.0 fusion.47
  89.2 0.4 fusion.46
  89.6 0.4 fusion.48
  90.0 1.0 fusion.47
  91.1 0.4 fusion.46
  91.9 1.0 fusion.47
  93.0 0.4 fusion.46
  93.8 1.0 fusion.47
  94.9 0.4 fusion.46
  95.7 1.0 fusion.47
  96.7 0.4 fusion.46
  97.6 1.0 fusion.47
  98.6 0.4 fusion.46
  99.5 1.0 fusion.47
  100.5 0.4 fusion.46
  101.4 1.0 fusion.47
  102.4 0.4 fusion.46
  103.2 1.0 fusion.47
  104.3 0.4 fusion.46
  104.7 0.4 fusion.48
  105.1 1.0 fusion.47
  106.1 2.5 %copy.10 = f32[2,64,64,128]{3,2,1,0:T(8,128)S(1)} copy(f32[2,64,64,128]{3,2,0,1:T(8,128)} %bitcast.51) | data formatting | bytes 8388608 | tf_op jit(solution)/shard_map/transpose | solution.py:53
  108.6 8.2 %all_to_all.31 = f32[2,64,64,128]{3,2,1,0:T(8,128)} all-to-all(f32[2,64,64,128]{3,2,1,0:T(8,128)S(1)} %copy.10), channel_id=1, replica_groups=mesh['pages_0'=2,'pages_1'=4,'pages_2'=8,'pages_3'=2,'tok'=2] {'pages_3'}, dimensions={0} | all-to-all | bytes 8388608 | tf_op jit(solution)/shard_map/all_to_all | solution.py:58
  116.8 2.8 %reduce_sum.61 = f32[64,64,128]{2,1,0:T(8,128)S(1)} reduce(f32[2,64,64,128]{3,2,1,0:T(8,128)} %all_to_all.31, f32[]{:T(128)} %constant.119.clone.1), dimensions={0}, to_apply=%region_7.8 | reduce | flops 524288 | bytes 6291460 | tf_op jit(solution)/shard_map/reduce_sum | solution.py:59
  119.6 56.9 %all_to_all.32 = f32[64,64,128]{2,1,0:T(8,128)} all-to-all(f32[64,64,128]{2,1,0:T(8,128)S(1)} %reduce_sum.61), channel_id=1, replica_groups=mesh['pages_0'=2,'pages_1'=4,'pages_2'=8,'pages_3'=2,'tok'=2] {'pages_0'..., dimensions={0} | all-to-all | bytes 4194304 | tf_op jit(solution)/shard_map/all_to_all | solution.py:66
  176.5 1.7 reduce_sum.62
  178.3 0.6 broadcast_in_dim.116
  178.9 3.3 %all-to-all-start.5 = ((f32[2,64,128]{2,1,0:T(8,128)}), f32[2,64,128]{2,1,0:T(8,128)S(1)}, u32[]{:S(2)}, u32[]{:S(2)}) async-start(f32[2,64,128]{2,1,0:T(8,128)} %broadcast_in_dim.116), calls=%async_computation.5 | async-start | bytes 131072 | tf_op jit(solution)/shard_map/all_to_all | solution.py:21
  182.2 0.7 broadcast_multiply_fusion
  182.9 4.9 %all-to-all-done.5 = f32[2,64,128]{2,1,0:T(8,128)S(1)} async-done(((f32[2,64,128]{2,1,0:T(8,128)}), f32[2,64,128]{2,1,0:T(8,128)S(1)}, u32[]{:S(2)}, u32[]{:S(2)}) %all-to-all-start.5) | async-done | bytes 65568 | tf_op jit(solution)/shard_map/all_to_all | solution.py:21
  187.8 0.6 reduce_sum.63
  (132 shorter events, 13.7 us)
Async XLA Ops:
  2.6 42.6 %all-to-all-start = ((bf16[64,2,32,128]{3,2,1,0:T(8,128)(2,1)}), bf16[64,2,32,128]{3,2,1,0:T(8,128)(2,1)S(1)}, u32[]{:S(2)}, u32[]{:S(2)}) async-start(bf16[64,2,32,128]{3,2,1,0:T(8,128)(2,1)} %broadcast_in_dim.109), calls=%async_computation | async-start | bytes 2097152 | tf_op jit(solution)/shard_map/all_to_all | solution.py:21
  51.1 0.9 copy-start
  52.1 20.9 %copy-start.1 = (s32[256,1]{0,1:T(1,128)S(1)}, s32[256,1]{0,1:T(1,128)}, u32[]{:S(2)}) copy-start(s32[256,1]{0,1:T(1,128)} %param.11) | copy-start | bytes 3076
  62.2 9.2 %all-to-all-start.2 = ((f32[2,8192,1]{1,2,0:T(1,128)}), f32[2,8192,1]{1,2,0:T(1,128)S(1)}, u32[]{:S(2)}, u32[]{:S(2)}) async-start(f32[2,8192,1]{1,2,0:T(1,128)} %broadcast_in_dim.113), calls=%async_computation.2 | async-start | bytes 131072 | tf_op jit(solution)/shard_map/all_to_all | solution.py:21
  178.9 8.9 %all-to-all-start.5 = ((f32[2,64,128]{2,1,0:T(8,128)}), f32[2,64,128]{2,1,0:T(8,128)S(1)}, u32[]{:S(2)}, u32[]{:S(2)}) async-start(f32[2,64,128]{2,1,0:T(8,128)} %broadcast_in_dim.116), calls=%async_computation.5 | async-start | bytes 131072 | tf_op jit(solution)/shard_map/all_to_all | solution.py:21
where the time goes:
time: 190 us; the launch traced here: 188 us
  blocking collectives  70.5 us (37%)
  waiting for transfers between devices  39.4 us (21%)
  matrix products  34.4 us (18%)
  starting transfers between devices  19.9 us (10%)
  other arithmetic  11.5 us (6%)
  local copies, waits for them, and re-layouts  10.5 us (6%)
    all_to_all x1, blocking collectives, sum_in_two_steps(): lax.all_to_all(nearer, far, split_axis=0, concat_axis=0, tiled=True)  56.9 us
    all_to_all x3, waiting for transfers between devices, from_everyone(): lax.all_to_all(jnp.broadcast_to(value[None], (length, *value.shape)), axi...  39.4 us
    all_to_all x3, starting transfers between devices, from_everyone(): lax.all_to_all(jnp.broadcast_to(value[None], (length, *value.shape)), axi...  19.9 us
    dot_general x16, matrix products, backward_block(): summed = jnp.dot(scaled, pages[0], preferred_element_type=jnp.float32)  16.2 us
    dot_general x32, matrix products, scores_for(): lax.dot_general(query_block, pages[page_no], (((1,), (1,)), ((), ())), pr...  12.1 us
    all_to_all x1, blocking collectives, sent_and_summed(): tiles = lax.all_to_all(split_up(value, dim, length), axis, 0, 0, tiled=True)  8.17 us
    dot_general x16, matrix products, backward_block(): lax.dot_general(scaled, query_block, (((0,), (0,)), ((), ())), preferred_...  6.01 us
    all_to_all x1, blocking collectives, from_everyone(): lax.all_to_all(jnp.broadcast_to(value[None], (length, *value.shape)), axi...  5.42 us
  transfers between devices with their start and end apart: 3, of which 3 were waited for; matrix products, arithmetic and copies ran while one was open for 0% of the time, Pallas kernels for 0%

commit v1 on v0

v1 whole, which is shorter than its diff:
```python
import functools
import math

import jax
import jax.numpy as jnp
from jax import lax
from jax.experimental import pallas as pl
from jax.experimental.pallas import tpu as pltpu
from jax.sharding import Mesh
from jax.sharding import PartitionSpec as P

MESH = pl.DeviceIdType.MESH
PAGES = ("yl", "x", "z", "core")

MASKED = -1.0e9
LOGIT_SPAN = 8.0
CENTRE_SHIFT = 0.5
FILL_SHARE = 0.75

NX, NZ = 4, 8
E, LQ, LP = 128, 32, 1024
HALF = LP // 2
ROWS = NZ * LQ
TILE = 256
F32, BF16 = jnp.float32, jnp.bfloat16

AUX, SIB_PAGE, FAR_PAGE, SIB_FAR_PAGE, TILE_Y = range(5)
TILE_Z = 5
TILE_Z_OTHER = TILE_Z + NZ
OWN_R, OWN_L, OTHER_R, OTHER_L, FWD_R, FWD_L = range(TILE_Z_OTHER + NZ, TILE_Z_OTHER + NZ + 6)
SUM_A, SUM_B, SUM_AR, SUM_BL, SUM_BR, SUM_AL, SUM_Y = range(FWD_L + 1, FWD_L + 8)
SUM_Z = SUM_Y + 1
FINAL_Q = SUM_Z + NZ
PG_FAR, PG_NEAR, LOSS_SIB, PG_Y, LOSS_Y = range(FINAL_Q + 1, FINAL_Q + 6)
COPIES = LOSS_Y + 1


def rows_of(pieces, shape):
    row = lax.broadcasted_iota(jnp.int32, shape, 0)
    total = jnp.zeros(shape, F32)
    for index, piece in enumerate(pieces):
        total = jnp.where(row == index, piece, total)
    return total


def dot(left, right, dims):
    return lax.dot_general(left, right, (dims, ((), ())), preferred_element_type=F32)


def kernel(
    q_ref, page_ref, pad_ref, label_ref,
    qg_ref, pg_ref, loss_ref,
    q_all, p_all, p_turned, bias, aux, aux_sib, labels_wide, group_ones,
    raw, weights, pg_sum, loss_sum,
    qg, in_a, in_b, in_left, in_right, in_y, turned, in_z, fin, in_fin,
    pg_sib, pg_out, pg_far, loss_out, loss_sib, loss_far,
    send_sem, recv_sem,
):
    yl, x, z = lax.axis_index("yl"), lax.axis_index("x"), lax.axis_index("z")
    core, yh = lax.axis_index("core"), lax.axis_index("yh")
    oyl, ocore, oyh = 1 - yl, 1 - core, 1 - yh
    right, left, across = lax.rem(x + 1, NX), lax.rem(x + 3, NX), lax.rem(x + 2, NX)

    def zplus(step):
        return lax.rem(z + step, NZ)

    def copy(source, target, index, where):
        return pltpu.make_async_remote_copy(
            src_ref=source,
            dst_ref=target,
            send_sem=send_sem.at[index],
            recv_sem=recv_sem.at[index],
            device_id=where,
            device_id_type=MESH,
        )

    to_sib, to_far, to_y = {"core": ocore}, {"yh": oyh}, {"yl": oyl}
    to_right, to_left = {"x": right}, {"x": left}

    barrier = pltpu.get_barrier_semaphore()
    partners = [to_sib, to_far, to_y, to_right, to_left]
    partners += [{"z": zplus(step)} for step in range(1, NZ)]
    for where in partners:
        pl.semaphore_signal(barrier, inc=1, device_id=where, device_id_type=MESH)

    own, other = yl * NX + x, oyl * NX + x
    q_all[own, z] = q_ref[yh]
    p_all[core, yh] = page_ref[0]
    row = lax.broadcasted_iota(jnp.int32, (8, 2 * E), 0)
    aux[...] = jnp.where(row == 0, label_ref[...].astype(F32), pad_ref[0].astype(F32))
    pl.semaphore_wait(barrier, len(partners))

    c_tile_y = copy(q_all.at[own, z], q_all.at[own, z], TILE_Y, to_y)
    c_tile_z = [
        copy(q_all.at[own, z], q_all.at[own, z], TILE_Z + step, {"z": zplus(step)})
        for step in range(1, NZ)
    ]
    c_tile_zo = [
        copy(q_all.at[other, z], q_all.at[other, z], TILE_Z_OTHER + step, {"z": zplus(step)})
        for step in range(1, NZ)
    ]
    c_far_page = copy(p_all.at[core, yh], p_all.at[core, yh], FAR_PAGE, to_far)
    c_sib_page = copy(p_all.at[core, yh], p_all.at[core, yh], SIB_PAGE, to_sib)
    c_sib_far = copy(p_all.at[core, oyh], p_all.at[core, oyh], SIB_FAR_PAGE, to_sib)
    c_aux = copy(aux, aux_sib, AUX, to_sib)
    c_own_r = copy(q_all.at[own], q_all.at[own], OWN_R, to_right)
    c_own_l = copy(q_all.at[own], q_all.at[own], OWN_L, to_left)
    c_other_r = copy(q_all.at[other], q_all.at[other], OTHER_R, to_right)
    c_other_l = copy(q_all.at[other], q_all.at[other], OTHER_L, to_left)
    from_left, from_right = yl * NX + left, oyl * NX + right
    c_fwd_r = copy(q_all.at[from_left], q_all.at[from_left], FWD_R, to_right)
    c_fwd_l = copy(q_all.at[from_right], q_all.at[from_right], FWD_L, to_left)

    c_tile_y.start()
    for each in c_tile_z:
        each.start()
    c_far_page.start()
    c_sib_page.start()
    c_aux.start()
    c_tile_y.wait_recv()
    for each in c_tile_zo:
        each.start()

    lane = lax.broadcasted_iota(jnp.int32, (2 * E, ROWS), 1)
    line = lax.broadcasted_iota(jnp.int32, (2 * E, ROWS), 0)
    group_ones[...] = (line // LQ == lane // LQ).astype(F32).astype(BF16)
    c_aux.wait_recv()
    position = lax.broadcasted_iota(jnp.int32, (LP, E), 0)
    wanted = (line % LQ == (lane // LQ) * 4 + 2 * core + yh).astype(F32).astype(BF16)
    block_row = lax.broadcasted_iota(jnp.int32, (8, 2 * E), 0)
    block_of = lax.broadcasted_iota(jnp.int32, (8, 2 * E), 1) // LQ
    for place, holder in ((core, aux), (ocore, aux_sib)):
        pad = holder[1:2, 0:E].astype(jnp.int32)
        bias[place] = jnp.where(position < LP - pad, 0.0, MASKED)
        spread = jnp.where(block_row == block_of, holder[0:1, :], 0.0).astype(BF16)
        labels_wide[place] = dot(spread, wanted, ((1,), (0,)))
    pg_sum[...] = jnp.zeros_like(pg_sum)
    loss_sum[...] = jnp.zeros_like(loss_sum)

    for each in c_tile_z:
        each.wait_recv()
    c_own_r.start()
    c_own_l.start()
    for each in c_tile_zo:
        each.wait_recv()
    c_other_r.start()
    c_other_l.start()
    c_far_page.wait_recv()
    c_sib_far.start()
    c_own_r.wait_recv()
    c_fwd_r.start()
    c_other_l.wait_recv()
    c_fwd_l.start()
    c_sib_page.wait_recv()
    c_sib_far.wait_recv()
    for place in range(2):
        for half in range(2):
            turned_half = p_all[place, half].astype(F32).T
            p_turned[place, :, half * HALF : (half + 1) * HALF] = turned_half.astype(BF16)
    c_own_l.wait_recv()
    c_other_r.wait_recv()
    c_fwd_r.wait_recv()
    c_fwd_l.wait_recv()

    score_scale = E ** (-0.5)
    power = score_scale * math.log2(math.e)
    gain = LOGIT_SPAN / LQ
    centre = LQ * (CENTRE_SHIFT + math.log(FILL_SHARE * LP))

    c_sum_a = copy(qg.at[0], in_a, SUM_A, to_right)
    c_sum_b = copy(qg.at[1], in_b, SUM_B, to_left)
    c_sum_ar = copy(qg.at[2], in_left.at[0], SUM_AR, to_right)
    c_sum_bl = copy(qg.at[3], in_right.at[1], SUM_BL, to_left)
    c_sum_br = copy(qg.at[4], in_left.at[1], SUM_BR, to_right)
    c_sum_al = copy(qg.at[5], in_right.at[0], SUM_AL, to_left)
    c_sum_y = copy(qg.at[6], in_y, SUM_Y, to_y)

    def block(step, carry):
        owner_x = jnp.where(
            step < 2,
            across,
            jnp.where(step >= 6, x, jnp.where((step == 2) | (step == 4), right, left)),
        )
        owner_y = jnp.where((step == 0) | (step == 2) | (step == 5) | (step == 7), yl, oyl)
        chunk = owner_y * NX + owner_x
        rows = q_all[chunk].reshape(ROWS, E)

        tops = []
        for place in range(2):
            top = jnp.full((8, ROWS), -3.0e38, F32)
            for tile in range(LP // TILE):
                span = pl.ds(tile % (HALF // TILE) * TILE, TILE)
                scores = dot(p_all[place, tile * TILE // HALF, span], rows, ((1,), (1,)))
                hidden = bias[place, tile * TILE : (tile + 1) * TILE]
                scores = scores + jnp.concatenate([hidden, hidden], axis=1)
                raw[place, tile * TILE : (tile + 1) * TILE] = scores
                top = jnp.maximum(top, jnp.max(scores.reshape(TILE // 8, 8, ROWS), axis=0))
            tops.append(jnp.max(top, axis=0, keepdims=True))
        sums = []
        for place in range(2):
            total = jnp.zeros((8, ROWS), F32)
            for tile in range(LP // TILE):
                span = slice(tile * TILE, (tile + 1) * TILE)
                weight = jnp.exp2((raw[place, span] - tops[place]) * power)
                weights[place, span] = weight.astype(BF16)
                total = total + jnp.sum(weight.reshape(TILE // 8, 8, ROWS), axis=0)
            sums.append(jnp.sum(total, axis=0, keepdims=True))

        top2, sum2 = rows_of(tops, (8, ROWS)), rows_of(sums + [1.0] * 6, (8, ROWS))
        smooth = top2 * score_scale + jnp.log(sum2)
        high = smooth.astype(BF16)
        rest = smooth - high.astype(F32)
        middle = rest.astype(BF16)
        low = (rest - middle.astype(F32)).astype(BF16)
        ones = group_ones[...]
        similarity = (
            dot(low, ones, ((1,), (0,))) + dot(middle, ones, ((1,), (0,)))
        ) + dot(high, ones, ((1,), (0,)))
        label_rows = [labels_wide[place, pl.ds(chunk, 1)] for place in range(2)]
        sign = 2.0 * rows_of(label_rows, (8, ROWS)) - 1.0
        lean = -sign * (gain * (similarity - centre))
        small = jnp.exp(-jnp.abs(lean))
        loss_sum[...] += jnp.maximum(lean, 0.0) + jnp.log1p(small)
        slope = -gain * sign * (jnp.where(lean >= 0.0, 1.0, small) / (1.0 + small))
        factor = slope / sum2
        columns = factor.T

        gradient = jnp.zeros((E, ROWS), F32)
        rows32 = rows.astype(F32)
        for place in range(2):
            gradient = gradient + factor[place : place + 1] * dot(
                p_turned[place], weights[place], ((1,), (0,))
            )
            scaled = (rows32 * columns[:, place : place + 1]).astype(BF16)
            pg_sum[place] += dot(weights[place], scaled, ((1,), (0,)))
        qg[step] = gradient

        @pl.when(step == 0)
        def _():
            c_sum_a.start()

        @pl.when(step == 1)
        def _():
            c_sum_b.start()

        @pl.when(step == 2)
        def _():
            c_sum_a.wait_recv()
            qg[2] += in_a[...]
            c_sum_ar.start()

        @pl.when(step == 3)
        def _():
            c_sum_b.wait_recv()
            qg[3] += in_b[...]
            c_sum_bl.start()

        @pl.when(step == 4)
        def _():
            c_sum_br.start()

        @pl.when(step == 5)
        def _():
            c_sum_al.start()

        @pl.when(step == 6)
        def _():
            c_sum_bl.wait_recv()
            c_sum_br.wait_recv()
            qg[6] += in_left[1] + in_right[1]
            c_sum_y.start()

        return carry

    lax.fori_loop(0, 8, block, 0)

    near, far = pl.ds(yh * HALF, HALF), pl.ds(oyh * HALF, HALF)
    c_pg_far = copy(pg_sum.at[ocore, far], pg_sib.at[0], PG_FAR, to_sib)
    c_pg_near = copy(pg_sum.at[ocore, near], pg_sib.at[1], PG_NEAR, to_sib)
    c_loss_sib = copy(loss_out.at[0], loss_sib, LOSS_SIB, to_sib)
    c_pg_y = copy(pg_out, pg_far, PG_Y, to_far)
    c_loss_y = copy(loss_out.at[1], loss_far, LOSS_Y, to_far)
    c_pg_far.start()
    c_pg_near.start()
    mark = lax.broadcasted_iota(jnp.int32, (8, ROWS), 1) % LQ == 0
    losses = jnp.sum(jnp.where(mark, loss_sum[...], 0.0), axis=1, keepdims=True)
    first, second = losses[0:1], losses[1:2]
    own_loss = jnp.where(core == 0, first, second)
    sib_loss = jnp.where(core == 0, second, first)
    loss_out[0] = jnp.broadcast_to(sib_loss, (8, E))
    c_loss_sib.start()

    c_sum_ar.wait_recv()
    c_sum_al.wait_recv()
    c_sum_y.wait_recv()
    total = ((qg[7] + in_left[0]) + (in_right[0] + in_y[...])) * score_scale
    for part in range(2):
        turned[part * 4 : part * 4 + 4] = total[:, part * E : (part + 1) * E].T.reshape(4, LQ, E)
    c_sum_z = [
        copy(turned.at[zplus(step)], in_z.at[step], SUM_Z + step, {"z": zplus(step)})
        for step in range(1, NZ)
    ]
    for each in c_sum_z:
        each.start()

    c_pg_far.wait_recv()
    pg_out[...] = pg_sum[core, far] + pg_sib[0]
    c_pg_y.start()
    c_loss_sib.wait_recv()
    loss_out[1] = jnp.broadcast_to(own_loss, (8, E)) + loss_sib[...]
    c_loss_y.start()

    for each in c_sum_z:
        each.wait_recv()
    mine = turned[z]
    for step in range(1, NZ):
        mine = mine + in_z[step]
    fin[...] = mine
    c_fin = copy(fin, in_fin, FINAL_Q, to_far)
    c_fin.start()
    qg_ref[yh] = mine
    c_pg_near.wait_recv()
    near_sum = pg_sum[core, near] + pg_sib[1]
    c_fin.wait_recv()
    qg_ref[oyh] = in_fin[...]
    c_loss_y.wait_recv()
    loss_ref[0] = jnp.max(loss_out[1, 0:1, 0:1] + loss_far[0:1, 0:1])
    c_pg_y.wait_recv()
    pg_ref[0] = (near_sum + pg_far[...]) * score_scale

    sent = [c_tile_y, c_far_page, c_sib_page, c_sib_far, c_aux, c_own_r, c_own_l, c_other_r]
    sent += [c_other_l, c_fwd_r, c_fwd_l, *c_tile_z, *c_tile_zo]
    sent += [c_sum_a, c_sum_b, c_sum_ar, c_sum_bl, c_sum_br, c_sum_al, c_sum_y, *c_sum_z]
    sent += [c_fin, c_pg_far, c_pg_near, c_loss_sib, c_pg_y, c_loss_y]
    for each in sent:
        each.wait_send()


def on_device(queries, pages, pad_counts, labels):
    vmem = pl.BlockSpec(memory_space=pltpu.VMEM)
    smem = pl.BlockSpec(memory_space=pltpu.SMEM)
    scratch = [
        pltpu.VMEM((8, NZ, LQ, E), BF16),
        pltpu.VMEM((2, 2, HALF, E), BF16),
        pltpu.VMEM((2, E, LP), BF16),
        pltpu.VMEM((2, LP, E), F32),
        pltpu.VMEM((8, 2 * E), F32),
        pltpu.VMEM((8, 2 * E), F32),
        pltpu.VMEM((2, 8, ROWS), F32),
        pltpu.VMEM((2 * E, ROWS), BF16),
        pltpu.VMEM((2, LP, ROWS), F32),
        pltpu.VMEM((2, LP, ROWS), BF16),
        pltpu.VMEM((2, LP, E), F32),
        pltpu.VMEM((8, ROWS), F32),
        pltpu.VMEM((8, E, ROWS), F32),
        pltpu.VMEM((E, ROWS), F32),
        pltpu.VMEM((E, ROWS), F32),
        pltpu.VMEM((2, E, ROWS), F32),
        pltpu.VMEM((2, E, ROWS), F32),
        pltpu.VMEM((E, ROWS), F32),
        pltpu.VMEM((NZ, LQ, E), F32),
        pltpu.VMEM((NZ, LQ, E), F32),
        pltpu.VMEM((LQ, E), F32),
        pltpu.VMEM((LQ, E), F32),
        pltpu.VMEM((2, HALF, E), F32),
        pltpu.VMEM((HALF, E), F32),
        pltpu.VMEM((HALF, E), F32),
        pltpu.VMEM((2, 8, E), F32),
        pltpu.VMEM((8, E), F32),
        pltpu.VMEM((8, E), F32),
        pltpu.SemaphoreType.DMA((COPIES,)),
        pltpu.SemaphoreType.DMA((COPIES,)),
    ]
    flops = 3 * 2 * (8 * ROWS) * (2 * LP) * E
    return pl.pallas_call(
        kernel,
        out_shape=(
            jax.ShapeDtypeStruct(queries.shape, F32),
            jax.ShapeDtypeStruct(pages.shape, F32),
            jax.ShapeDtypeStruct((1,), F32),
        ),
        in_specs=[vmem, vmem, smem, vmem],
        out_specs=(vmem, vmem, smem),
        scratch_shapes=scratch,
        compiler_params=pltpu.CompilerParams(
            collective_id=0, has_side_effects=True, vmem_limit_bytes=48 * 1024 * 1024
        ),
        cost_estimate=pl.CostEstimate(
            flops=flops, bytes_accessed=2 << 20, transcendentals=8 * ROWS * 2 * LP
        ),
    )(queries, pages, pad_counts, labels.reshape(1, -1))


def solution(mesh):
    finer = Mesh(mesh.devices.reshape(2, NX, NZ, 2, 2), (*PAGES, "yh"))
    return jax.shard_map(
        on_device,
        mesh=finer,
        in_specs=(P(PAGES, None, None), P(PAGES, "yh", None), P(PAGES), P(None, PAGES)),
        out_specs=(P(PAGES, None, None), P(PAGES, "yh", None), P(PAGES)),
        check_vma=False,
    )
```

time: 190 us -> 60.6 us (0.32)
  blocking collectives: 70.5 us -> 0 us
  Pallas kernels: 0 us -> 53.7 us
  waiting for transfers between devices: 39.4 us -> 0 us
  matrix products: 34.4 us -> 0 us
  starting transfers between devices: 19.9 us -> 0 us
  other arithmetic: 11.5 us -> 0 us
  local copies, waits for them, and re-layouts: 10.5 us -> 3.61 us
    all_to_all x3 -> x0, blocking collectives: 70.5 us -> none  [the longest x1 56.9 us: sum_in_two_steps(): lax.all_to_all(nearer, far, split_axis=0, concat_axis=0, tiled=True)]
    pallas_call x0 -> x1, Pallas kernels: none -> 53.7 us  [on_device(): pl.pallas_call(kernel, out_shape=(jax.ShapeDtypeStruct(queries.shape, F32...]
    all_to_all x3 -> x0, waiting for transfers between devices: 39.4 us -> none  [from_everyone(): lax.all_to_all(jnp.broadcast_to(value[None], (length, *value.shape)), axi...]
    dot_general x64 -> x0, matrix products: 34.4 us -> none  [the longest x16 16.2 us: backward_block(): summed = jnp.dot(scaled, pages[0], preferred_element_type=jnp.float32)]
    all_to_all x3 -> x0, starting transfers between devices: 19.9 us -> none  [from_everyone(): lax.all_to_all(jnp.broadcast_to(value[None], (length, *value.shape)), axi...]
    reduce_sum x21 -> x0, other arithmetic: 9.01 us -> none  [the longest x16 3.14 us: forward_block(): jnp.sum(jnp.exp(scores - highest[:, None]), axis=1)]
    broadcast_in_dim x8 -> x0, local copies, waits for them, and re-layouts: 6.19 us -> none  [the longest x4 3.76 us: from_everyone(): jnp.broadcast_to(value[None], (length, *value.shape))]
    unnamed x4 -> x8, local copies, waits for them, and re-layouts: 0.42 us -> 3.61 us
  transfers between devices with their start and end apart: 3 -> 0, of which waited for: 3 -> 0; matrix products, arithmetic and copies ran while one was open for 0% -> 0% of each run, Pallas kernels for 0% -> 0%
where the time goes in v1:
time: 60.6 us; the launch traced here: 60.4 us
  Pallas kernels  53.7 us (89%)
  local copies, waits for them, and re-layouts  3.61 us (6%)
  between operations  3.03 us (5%)
    pallas_call x1, Pallas kernels, on_device(): pl.pallas_call(kernel, out_shape=(jax.ShapeDtypeStruct(queries.shape, F32...  53.7 us
    unnamed x8, local copies, waits for them, and re-layouts  3.61 us

profile of v1, /device:TPU:8, one launch (start us, length us, event | category | flops | bytes accessed | tf_op | source)
XLA Modules:
  0.0 60.4 jit_solution(10195027309260444082)
XLA Ops:
  1.3 0.0 copy-start.2
  1.3 0.7 %copy-done.2 = s32[256,1]{0,1:T(1,128)S(1)} copy-done((s32[256,1]{0,1:T(1,128)S(1)}, s32[256,1]{0,1:T(1,128)}, u32[]{:S(2)}) %copy-start.2) | copy-done | bytes 1048
  2.0 0.0 copy-start
  2.0 0.9 %copy-done = bf16[1,512,128]{2,1,0:T(8,128)(2,1)S(1)} copy-done((bf16[1,512,128]{2,1,0:T(8,128)(2,1)S(1)}, bf16[1,512,128]{2,1,0:T(8,128)(2,1)}, u32[]{:S(2)}) %copy-start) | copy-done | bytes 131096
  2.9 0.0 copy-start.1
  2.9 0.7 %copy-done.1 = bf16[2,32,128]{2,1,0:T(8,128)(2,1)S(1)} copy-done((bf16[2,32,128]{2,1,0:T(8,128)(2,1)S(1)}, bf16[2,32,128]{2,1,0:T(8,128)(2,1)}, u32[]{:S(2)}) %copy-start.1) | copy-done | bytes 16408
  3.6 53.7 %shard_map.67 = (f32[2,32,128]{2,1,0:T(8,128)S(1)}, f32[1,512,128]{2,1,0:T(8,128)S(1)}, f32[1]{0:T(128)}) custom-call(bf16[2,32,128]{2,1,0:T(8,128)(2,1)S(1)} %copy-done.1, bf16[1,512,128]{2,1,0:T(8,128)(2,1)S(1)} %copy-done, s32[1]{0:T(128)S(6)} %copy.10.pad_ref, s32[1,256]{1,0:T(1,128)S(1)} %bitcast.1), custom_call_target="tpu_custom_call" | custom-call | flops 3221225472 | bytes 2097152 | tf_op jit(solution)/shard_map/pallas_call | solution.py:375
  57.3 0.6 %copy.11 = f32[2,32,128]{2,1,0:T(8,128)} copy(f32[2,32,128]{2,1,0:T(8,128)S(1)} %get-tuple-element.6) | data formatting | bytes 65536
  57.9 0.7 %copy.12 = f32[1,512,128]{2,1,0:T(8,128)} copy(f32[1,512,128]{2,1,0:T(8,128)S(1)} %get-tuple-element.7) | data formatting | bytes 524288
Async XLA Ops:
  1.3 0.7 %copy-start.2 = (s32[256,1]{0,1:T(1,128)S(1)}, s32[256,1]{0,1:T(1,128)}, u32[]{:S(2)}) copy-start(s32[256,1]{0,1:T(1,128)} %param.7) | copy-start | bytes 3076
  2.0 0.9 %copy-start = (bf16[1,512,128]{2,1,0:T(8,128)(2,1)S(1)}, bf16[1,512,128]{2,1,0:T(8,128)(2,1)}, u32[]{:S(2)}) copy-start(bf16[1,512,128]{2,1,0:T(8,128)(2,1)} %page_ref.1) | copy-start | bytes 393220
  2.9 0.7 %copy-start.1 = (bf16[2,32,128]{2,1,0:T(8,128)(2,1)S(1)}, bf16[2,32,128]{2,1,0:T(8,128)(2,1)}, u32[]{:S(2)}) copy-start(bf16[2,32,128]{2,1,0:T(8,128)(2,1)} %q_ref.1) | copy-start | bytes 49156

commit v2 on v1

v2 whole, which is shorter than its diff:
```python
import math

import jax
import jax.numpy as jnp
from jax import lax
from jax.experimental import pallas as pl
from jax.experimental.pallas import tpu as pltpu
from jax.sharding import Mesh
from jax.sharding import PartitionSpec as P

MESH = pl.DeviceIdType.MESH
PAGES = ("yl", "x", "z", "core")

MASKED = -1.0e9
LOGIT_SPAN = 8.0
CENTRE_SHIFT = 0.5
FILL_SHARE = 0.75

NX, NZ = 4, 8
E, LQ, LP = 128, 32, 1024
HALF = LP // 2
ROWS = NX * 2 * LQ
ALL = NZ * ROWS
TILE = 256
F32, BF16 = jnp.float32, jnp.bfloat16

AUX, SIB_PAGE, TILE_Y, FAR_PAGE, SIB_FAR = 0, 1, 2, 3, 5
TILE_Z, TILE_X = 7, 7 + NZ
SUM_X, SUM_Z = TILE_X + NZ, TILE_X + 2 * NZ
FINAL = SUM_Z + NZ
PG_FAR, PG_NEAR, PG_Y, LOSS_SIB, LOSS_Y = range(FINAL + 3, FINAL + 8)
COPIES = LOSS_Y + 1


def dot(left, right, dims=((1,), (0,))):
    return lax.dot_general(left, right, (dims, ((), ())), preferred_element_type=F32)


def offset(rank):
    half, odd = (rank + 1) // 2, rank % 2
    return (odd * half + (1 - odd) * (NZ - half)) % NZ


def kernel(
    q_ref, page_ref, pad_ref, label_ref,
    qg_ref, pg_ref, loss_ref,
    q_all, p_all, p_turned, bias, labels, aux, aux_sib, labels_wide, group_ones,
    raw, weights, tops, sums, labels_rank, scaled, factors, pg_sum,
    qg, qg_sent, in_x, out_z, in_z, fin, in_fin,
    pg_sib, pg_out, pg_far, loss_out, loss_sib, loss_far,
    load_sem, send_sem, recv_sem,
):
    yl, x, z = lax.axis_index("yl"), lax.axis_index("x"), lax.axis_index("z")
    core, yh = lax.axis_index("core"), lax.axis_index("yh")
    oyl, ocore, oyh = 1 - yl, 1 - core, 1 - yh

    loads = [
        pltpu.make_async_copy(q_ref.at[yh], q_all.at[z, x, yl], load_sem.at[0]),
        pltpu.make_async_copy(page_ref.at[0], p_all.at[core, yh], load_sem.at[1]),
        pltpu.make_async_copy(label_ref, labels, load_sem.at[2]),
    ]
    for each in loads:
        each.start()

    def zplus(step):
        return (z + step) % NZ

    def xplus(step):
        return {"x": (x + step) % NX}

    def copy(source, target, index, where):
        return pltpu.make_async_remote_copy(
            src_ref=source,
            dst_ref=target,
            send_sem=send_sem.at[index],
            recv_sem=recv_sem.at[index],
            device_id=where,
            device_id_type=MESH,
        )

    to_sib, to_far, to_y = {"core": ocore}, {"yh": oyh}, {"yl": oyl}
    to_corner = {"yl": oyl, "yh": oyh}

    barrier = pltpu.get_barrier_semaphore()
    partners = [to_sib, to_far, to_y, to_corner]
    partners += [xplus(step) for step in range(1, NX)]
    partners += [{"z": zplus(step)} for step in range(1, NZ)]
    for where in partners:
        pl.semaphore_signal(barrier, inc=1, device_id=where, device_id_type=MESH)

    lane = lax.broadcasted_iota(jnp.int32, (2 * E, ROWS), 1)
    line = lax.broadcasted_iota(jnp.int32, (2 * E, ROWS), 0)
    group_ones[...] = (line // LQ == lane // LQ).astype(F32).astype(BF16)
    for each in loads:
        each.wait()
    row = lax.broadcasted_iota(jnp.int32, (8, 2 * E), 0)
    aux[...] = jnp.where(row == 0, labels[...].astype(F32), pad_ref[0].astype(F32))
    pl.semaphore_wait(barrier, len(partners))

    own_tile = q_all.at[z, x, yl]
    c_tile_y = copy(own_tile, own_tile, TILE_Y, to_y)
    pair = q_all.at[z, x]
    c_tile_z = [
        copy(pair, pair, TILE_Z + rank, {"z": zplus(NZ - offset(rank))}) for rank in range(1, NZ)
    ]
    piece = HALF // 2
    c_far_page = []
    c_sib_far = []
    for part in range(2):
        mine = p_all.at[core, yh, pl.ds(part * piece, piece)]
        c_far_page.append(copy(mine, mine, FAR_PAGE + part, to_far))
        theirs = p_all.at[core, oyh, pl.ds(part * piece, piece)]
        c_sib_far.append(copy(theirs, theirs, SIB_FAR + part, to_sib))
    c_sib_page = copy(p_all.at[core, yh], p_all.at[core, yh], SIB_PAGE, to_sib)
    c_aux = copy(aux, aux_sib, AUX, to_sib)

    def send_x(rank):
        block = q_all.at[zplus(offset(rank)), x]
        for step in range(1, NX):
            copy(block, block, TILE_X + rank, xplus(step)).start()

    def three(rank):
        block = q_all.at[zplus(offset(rank)), pl.ds(0, NX - 1)]
        return copy(block, block, TILE_X + rank, xplus(1))

    c_tile_y.start()
    for each in c_far_page:
        each.start()
    c_aux.start()
    c_sib_page.start()
    c_tile_y.wait_recv()
    for each in c_tile_z:
        each.start()
    send_x(0)

    c_aux.wait_recv()
    position = lax.broadcasted_iota(jnp.int32, (LP, E), 0)
    number = (lane // LQ % 2 * NX + lane // (2 * LQ)) * (NZ * 4) + 2 * core + yh
    wanted = (line // (NZ * 4) == number // (NZ * 4)).astype(F32).astype(BF16)
    block_row = lax.broadcasted_iota(jnp.int32, (8, 2 * E), 0)
    place_in = lax.broadcasted_iota(jnp.int32, (8, 2 * E), 1) % (NZ * 4)
    for place, holder in ((core, aux), (ocore, aux_sib)):
        pad = holder[1:2, 0:E].astype(jnp.int32)
        bias[place] = jnp.where(position < LP - pad, 0.0, MASKED)
        chosen = place_in == block_row * 4 + 2 * core + yh
        spread = jnp.where(chosen, holder[0:1, :], 0.0).astype(BF16)
        labels_wide[place] = dot(spread, wanted)

    for rank in range(1, 3):
        c_tile_z[rank - 1].wait_recv()
        send_x(rank)
    c_sib_page.wait_recv()
    for place in range(2):
        near_half = pl.ds(pl.multiple_of(yh * HALF, HALF), HALF)
        p_turned[place, :, near_half] = p_all[place, yh].astype(F32).T.astype(BF16)
    for rank in range(3, 5):
        c_tile_z[rank - 1].wait_recv()
        send_x(rank)
    for part in range(2):
        c_far_page[part].wait_recv()
        c_sib_far[part].start()
    for part in range(2):
        c_sib_far[part].wait_recv()
    for place in range(2):
        far_half = pl.ds(pl.multiple_of(oyh * HALF, HALF), HALF)
        p_turned[place, :, far_half] = p_all[place, oyh].astype(F32).T.astype(BF16)

    score_scale = E ** (-0.5)
    power = score_scale * math.log2(math.e)
    gain = LOGIT_SPAN / LQ
    centre = LQ * (CENTRE_SHIFT + math.log(FILL_SHARE * LP))

    def forward(rank, carry):
        @pl.when(rank < 3)
        def _():
            later = rank + 5
            copy(pair, pair, TILE_Z + later, to_y).wait_recv()
            send_x(later)

        three(rank).wait_recv()
        block = zplus(offset(rank))
        lanes = pl.ds(pl.multiple_of(rank * ROWS, ROWS), ROWS)
        columns = q_all[block].reshape(ROWS, E).astype(F32).T.astype(BF16)
        for place in range(2):
            top = jnp.full((8, ROWS), -3.0e38, F32)
            for half in range(2):
                scores = dot(p_all[place, half], columns)
                hidden = bias[place, half * HALF : (half + 1) * HALF]
                scores = scores + jnp.concatenate([hidden, hidden], axis=1)
                raw[place, half * HALF : (half + 1) * HALF] = scores
                top = jnp.maximum(top, jnp.max(scores.reshape(HALF // 8, 8, ROWS), axis=0))
            tops[place, pl.ds(rank, 1)] = jnp.max(top, axis=0, keepdims=True)
        for place in range(2):
            total = jnp.zeros((8, ROWS), F32)
            top = tops[place, pl.ds(rank, 1)]
            for tile in range(LP // TILE):
                span = slice(tile * TILE, (tile + 1) * TILE)
                weight = jnp.exp2((raw[place, span] - top) * power)
                weights[place, span, lanes] = weight.astype(BF16)
                total = total + jnp.sum(weight.reshape(TILE // 8, 8, ROWS), axis=0)
            sums[place, pl.ds(rank, 1)] = jnp.sum(total, axis=0, keepdims=True)
        label_rows = [labels_wide[place, pl.ds(block, 1)] for place in range(2)]
        for place in range(2):
            labels_rank[place, pl.ds(rank, 1)] = label_rows[place]
        return carry

    lax.fori_loop(0, NZ, forward, 0)

    losses = []
    for place in range(2):
        smooth = tops[place] * score_scale + jnp.log(sums[place])
        high = smooth.astype(BF16)
        rest = smooth - high.astype(F32)
        middle = rest.astype(BF16)
        low = (rest - middle.astype(F32)).astype(BF16)
        ones = group_ones[...]
        similarity = (dot(low, ones) + dot(middle, ones)) + dot(high, ones)
        sign = 2.0 * labels_rank[place] - 1.0
        lean = -sign * (gain * (similarity - centre))
        small = jnp.exp(-jnp.abs(lean))
        losses.append(jnp.maximum(lean, 0.0) + jnp.log1p(small))
        slope = -gain * sign * (jnp.where(lean >= 0.0, 1.0, small) / (1.0 + small))
        factor = slope / sums[place]
        factors[place] = factor
        turned_factor = factor.T
        for rank in range(NZ):
            rows = q_all[zplus(offset(rank))].reshape(ROWS, E).astype(F32)
            rows = (rows * turned_factor[:, rank : rank + 1]).astype(BF16)
            scaled[place, rank * ROWS : (rank + 1) * ROWS] = rows

    def page_terms(place, half, tile):
        span = pl.ds(pl.multiple_of(half * HALF + tile * TILE, TILE), TILE)
        pg_sum[place, span] = dot(weights[place, span], scaled[place])

    near = pl.ds(pl.multiple_of(yh * HALF, HALF), HALF)
    far = pl.ds(pl.multiple_of(oyh * HALF, HALF), HALF)
    c_pg_far = copy(pg_sum.at[ocore, far], pg_sib.at[0], PG_FAR, to_sib)
    c_pg_near = copy(pg_sum.at[ocore, near], pg_sib.at[1], PG_NEAR, to_sib)
    c_loss_sib = copy(loss_out.at[0], loss_sib, LOSS_SIB, to_sib)
    c_pg_y = copy(pg_out, pg_far, PG_Y, to_far)
    c_loss_y = copy(loss_out.at[1], loss_far, LOSS_Y, to_far)

    for tile in range(HALF // TILE):
        page_terms(ocore, oyh, tile)
    c_pg_far.start()
    mark = lax.broadcasted_iota(jnp.int32, (8, ROWS), 1) % LQ == 0
    first, second = [jnp.sum(jnp.where(mark, each, 0.0), keepdims=True) for each in losses]
    own_loss = jnp.where(core == 0, first, second)
    sib_loss = jnp.where(core == 0, second, first)
    loss_out[0] = jnp.broadcast_to(sib_loss, (8, E))
    c_loss_sib.start()
    for tile in range(HALF // TILE):
        page_terms(core, oyh, tile)

    def backward(step, carry):
        rank = NZ - 1 - step
        lanes = pl.ds(pl.multiple_of(rank * ROWS, ROWS), ROWS)
        gradient = jnp.zeros((E, ROWS), F32)
        for place in range(2):
            gradient = gradient + factors[place, pl.ds(rank, 1)] * dot(
                p_turned[place], weights[place, :, lanes]
            )
        turned = gradient.T.reshape(NX, 2, LQ, E)
        qg[rank] = turned
        qg_sent[rank] = turned.astype(BF16)
        for step_x in range(1, NX):
            copy(
                qg_sent.at[rank, (x + step_x) % NX],
                in_x.at[rank, step_x - 1],
                SUM_X + rank,
                xplus(step_x),
            ).start()

        @pl.when(step == 1)
        def _():
            c_pg_far.wait_recv()
            pg_out[...] = pg_sum[core, far] + pg_sib[0]
            c_pg_y.start()
            c_loss_sib.wait_recv()
            loss_out[1] = jnp.broadcast_to(own_loss, (8, E)) + loss_sib[...]
            c_loss_y.start()

        return carry

    lax.fori_loop(0, NZ, backward, 0)
    def sum_x(step, carry):
        rank = NZ - 1 - step
        copy(qg_sent.at[rank, pl.ds(0, NX - 1)], in_x.at[rank], SUM_X + rank, xplus(1)).wait_recv()
        total = qg[rank, x]
        for slot in range(NX - 1):
            total = total + in_x[rank, slot].astype(F32)
        out_z[rank] = total

        @pl.when(rank > 0)
        def _():
            copy(out_z.at[rank], in_z.at[rank], SUM_Z + rank, {"z": zplus(offset(rank))}).start()

        @pl.when(step % 2 == 1)
        def _():
            late = step // 4
            page_terms(late * core + (1 - late) * ocore, yh, step // 2 % 2)

        @pl.when(step == 3)
        def _():
            c_pg_near.start()

        return carry

    lax.fori_loop(0, NZ, sum_x, 0)
    total = out_z[0]
    for rank in range(NZ - 1, 0, -1):
        copy(out_z.at[rank], in_z.at[rank], SUM_Z + rank, to_y).wait_recv()
        total = total + in_z[rank]
    fin[...] = total * score_scale
    c_fin = [
        copy(fin.at[yl], in_fin.at[2], FINAL + 2, to_far),
        copy(fin.at[oyl], in_fin.at[0], FINAL, to_y),
        copy(fin.at[oyl], in_fin.at[1], FINAL + 1, to_corner),
    ]
    for each in c_fin:
        each.start()
    c_pg_near.wait_recv()
    near_sum = pg_sum[core, near] + pg_sib[1]
    c_loss_y.wait_recv()
    loss_ref[0] = jnp.max(loss_out[1, 0:1, 0:1] + loss_far[0:1, 0:1])
    c_fin[1].wait_recv()
    qg_ref[yh] = fin[yl] + in_fin[0]
    c_fin[2].wait_recv()
    c_fin[0].wait_recv()
    qg_ref[oyh] = in_fin[2] + in_fin[1]
    c_pg_y.wait_recv()
    pg_ref[0] = (near_sum + pg_far[...]) * score_scale

    sent = [c_tile_y, *c_far_page, *c_sib_far, c_sib_page, c_aux, *c_tile_z, *c_fin]
    sent += [c_pg_far, c_pg_near, c_loss_sib, c_pg_y, c_loss_y]
    for each in sent:
        each.wait_send()
    for rank in range(NZ):
        three(rank).wait_send()
        copy(qg_sent.at[rank, pl.ds(0, NX - 1)], in_x.at[rank], SUM_X + rank, xplus(1)).wait_send()
        if rank:
            copy(out_z.at[rank], in_z.at[rank], SUM_Z + rank, to_y).wait_send()


def on_device(queries, pages, pad_counts, labels):
    vmem = pl.BlockSpec(memory_space=pltpu.VMEM)
    smem = pl.BlockSpec(memory_space=pltpu.SMEM)
    hbm = pl.BlockSpec(memory_space=pl.ANY)
    scratch = [
        pltpu.VMEM((NZ, NX, 2, LQ, E), BF16),
        pltpu.VMEM((2, 2, HALF, E), BF16),
        pltpu.VMEM((2, E, LP), BF16),
        pltpu.VMEM((2, LP, E), F32),
        pltpu.VMEM((1, 2 * E), jnp.int32),
        pltpu.VMEM((8, 2 * E), F32),
        pltpu.VMEM((8, 2 * E), F32),
        pltpu.VMEM((2, 8, ROWS), F32),
        pltpu.VMEM((2 * E, ROWS), BF16),
        pltpu.VMEM((2, LP, ROWS), F32),
        pltpu.VMEM((2, LP, ALL), BF16),
        pltpu.VMEM((2, NZ, ROWS), F32),
        pltpu.VMEM((2, NZ, ROWS), F32),
        pltpu.VMEM((2, NZ, ROWS), F32),
        pltpu.VMEM((2, ALL, E), BF16),
        pltpu.VMEM((2, NZ, ROWS), F32),
        pltpu.VMEM((2, LP, E), F32),
        pltpu.VMEM((NZ, NX, 2, LQ, E), F32),
        pltpu.VMEM((NZ, NX, 2, LQ, E), BF16),
        pltpu.VMEM((NZ, NX - 1, 2, LQ, E), BF16),
        pltpu.VMEM((NZ, 2, LQ, E), F32),
        pltpu.VMEM((NZ, 2, LQ, E), F32),
        pltpu.VMEM((2, LQ, E), F32),
        pltpu.VMEM((3, LQ, E), F32),
        pltpu.VMEM((2, HALF, E), F32),
        pltpu.VMEM((HALF, E), F32),
        pltpu.VMEM((HALF, E), F32),
        pltpu.VMEM((2, 8, E), F32),
        pltpu.VMEM((8, E), F32),
        pltpu.VMEM((8, E), F32),
        pltpu.SemaphoreType.DMA((3,)),
        pltpu.SemaphoreType.DMA((COPIES,)),
        pltpu.SemaphoreType.DMA((COPIES,)),
    ]
    flops = 3 * 2 * ALL * (2 * LP) * E
    return pl.pallas_call(
        kernel,
        out_shape=(
            jax.ShapeDtypeStruct(queries.shape, F32),
            jax.ShapeDtypeStruct(pages.shape, F32),
            jax.ShapeDtypeStruct((1,), F32),
        ),
        in_specs=[hbm, hbm, smem, hbm],
        out_specs=(vmem, vmem, smem),
        scratch_shapes=scratch,
        compiler_params=pltpu.CompilerParams(
            collective_id=0, has_side_effects=True, vmem_limit_bytes=56 * 1024 * 1024
        ),
        cost_estimate=pl.CostEstimate(
            flops=flops, bytes_accessed=2 << 20, transcendentals=ALL * 2 * LP
        ),
    )(queries, pages, pad_counts, labels.reshape(1, -1))


def solution(mesh):
    finer = Mesh(mesh.devices.reshape(2, NX, NZ, 2, 2), (*PAGES, "yh"))
    return jax.shard_map(
        on_device,
        mesh=finer,
        in_specs=(P(PAGES, None, None), P(PAGES, "yh", None), P(PAGES), P(None, PAGES)),
        out_specs=(P(PAGES, None, None), P(PAGES, "yh", None), P(PAGES)),
        check_vma=False,
    )
```

time: 60.6 us -> 52.5 us (0.87)
  the two profiles are of different devices: /device:TPU:8 before, /device:TPU:1 now
where the time goes in v2:
time: 52.5 us; the launch traced here: 52.3 us
  Pallas kernels  46.2 us (88%)
  between operations  3.1 us (6%)
  local copies, waits for them, and re-layouts  3.04 us (6%)
    pallas_call x1, Pallas kernels, on_device(): pl.pallas_call(kernel, out_shape=(jax.ShapeDtypeStruct(queries.shape, F32...  46.2 us
    unnamed x2, local copies, waits for them, and re-layouts  3.04 us

profile of v2, /device:TPU:1, one launch (start us, length us, event | category | flops | bytes accessed | tf_op | source)
XLA Modules:
  0.0 52.3 jit_solution(17748070292986568099)
XLA Ops:
  1.3 46.2 %shard_map.67 = (f32[2,32,128]{2,1,0:T(8,128)}, f32[1,512,128]{2,1,0:T(8,128)}, f32[1]{0:T(128)}) custom-call(bf16[2,32,128]{2,1,0:T(8,128)(2,1)} %q_ref.1, bf16[1,512,128]{2,1,0:T(8,128)(2,1)} %page_ref.1, s32[1]{0:T(128)S(6)} %copy.10.pad_ref, s32[1,256]{1,0:T(1,128)} %bitcast.1), custom_call_target="tpu_custom_call" | custom-call | flops 3221225472 | bytes 2097152 | tf_op jit(solution)/shard_map/pallas_call | solution.py:385
  47.4 1.4 %copy.11 = f32[2,32,128]{2,1,0:T(8,128)} copy(f32[2,32,128]{2,1,0:T(8,128)} %get-tuple-element.6) | data formatting | bytes 65536
  48.8 1.7 %copy.12 = f32[1,512,128]{2,1,0:T(8,128)} copy(f32[1,512,128]{2,1,0:T(8,128)} %get-tuple-element.7) | data formatting | bytes 524288

commit v3 on v2

--- a/solution.py
+++ b/solution.py
@@ -153,58 +153,62 @@
     for place in range(2):
         near_half = pl.ds(pl.multiple_of(yh * HALF, HALF), HALF)
         p_turned[place, :, near_half] = p_all[place, yh].astype(F32).T.astype(BF16)
+    c_far_page[0].wait_recv()
+    c_sib_far[0].start()
     for rank in range(3, 5):
         c_tile_z[rank - 1].wait_recv()
         send_x(rank)
-    for part in range(2):
-        c_far_page[part].wait_recv()
-        c_sib_far[part].start()
+    c_far_page[1].wait_recv()
+    c_sib_far[1].start()
+    for rank in range(5, NZ):
+        c_tile_z[rank - 1].wait_recv()
+        send_x(rank)
     for part in range(2):
         c_sib_far[part].wait_recv()
-    for place in range(2):
-        far_half = pl.ds(pl.multiple_of(oyh * HALF, HALF), HALF)
-        p_turned[place, :, far_half] = p_all[place, oyh].astype(F32).T.astype(BF16)
 
     score_scale = E ** (-0.5)
     power = score_scale * math.log2(math.e)
     gain = LOGIT_SPAN / LQ
     centre = LQ * (CENTRE_SHIFT + math.log(FILL_SHARE * LP))
 
-    def forward(rank, carry):
-        @pl.when(rank < 3)
-        def _():
-            later = rank + 5
-            copy(pair, pair, TILE_Z + later, to_y).wait_recv()
-            send_x(later)
-
+    def scores_of(rank):
         three(rank).wait_recv()
-        block = zplus(offset(rank))
-        lanes = pl.ds(pl.multiple_of(rank * ROWS, ROWS), ROWS)
-        columns = q_all[block].reshape(ROWS, E).astype(F32).T.astype(BF16)
+        rows = q_all[zplus(offset(rank))].reshape(ROWS, E)
+        found = []
         for place in range(2):
             top = jnp.full((8, ROWS), -3.0e38, F32)
             for half in range(2):
-                scores = dot(p_all[place, half], columns)
+                scores = dot(p_all[place, half], rows, ((1,), (1,)))
                 hidden = bias[place, half * HALF : (half + 1) * HALF]
                 scores = scores + jnp.concatenate([hidden, hidden], axis=1)
-                raw[place, half * HALF : (half + 1) * HALF] = scores
+                raw[rank % 2, place, half * HALF : (half + 1) * HALF] = scores
                 top = jnp.maximum(top, jnp.max(scores.reshape(HALF // 8, 8, ROWS), axis=0))
-            tops[place, pl.ds(rank, 1)] = jnp.max(top, axis=0, keepdims=True)
+            found.append(jnp.max(top, axis=0, keepdims=True))
+        return found
+
+    def weights_of(rank, found):
         for place in range(2):
+            tops[place, rank : rank + 1] = found[place]
             total = jnp.zeros((8, ROWS), F32)
-            top = tops[place, pl.ds(rank, 1)]
             for tile in range(LP // TILE):
                 span = slice(tile * TILE, (tile + 1) * TILE)
-                weight = jnp.exp2((raw[place, span] - top) * power)
-                weights[place, span, lanes] = weight.astype(BF16)
+                weight = jnp.exp2((raw[rank % 2, place, span] - found[place]) * power)
+                weights[place, span, rank * ROWS : (rank + 1) * ROWS] = weight.astype(BF16)
                 total = total + jnp.sum(weight.reshape(TILE // 8, 8, ROWS), axis=0)
-            sums[place, pl.ds(rank, 1)] = jnp.sum(total, axis=0, keepdims=True)
-        label_rows = [labels_wide[place, pl.ds(block, 1)] for place in range(2)]
+            sums[place, rank : rank + 1] = jnp.sum(total, axis=0, keepdims=True)
+
+    found = scores_of(0)
+    for rank in range(NZ):
+        following = scores_of(rank + 1) if rank + 1 < NZ else None
+        weights_of(rank, found)
+        found = following
+        if rank == 1:
+            for place in range(2):
+                far_half = pl.ds(pl.multiple_of(oyh * HALF, HALF), HALF)
+                p_turned[place, :, far_half] = p_all[place, oyh].astype(F32).T.astype(BF16)
+        label_rows = [labels_wide[place, pl.ds(zplus(offset(rank)), 1)] for place in range(2)]
         for place in range(2):
-            labels_rank[place, pl.ds(rank, 1)] = label_rows[place]
-        return carry
-
-    lax.fori_loop(0, NZ, forward, 0)
+            labels_rank[place, rank : rank + 1] = label_rows[place]
 
     losses = []
     for place in range(2):
@@ -222,11 +226,6 @@
         slope = -gain * sign * (jnp.where(lean >= 0.0, 1.0, small) / (1.0 + small))
         factor = slope / sums[place]
         factors[place] = factor
-        turned_factor = factor.T
-        for rank in range(NZ):
-            rows = q_all[zplus(offset(rank))].reshape(ROWS, E).astype(F32)
-            rows = (rows * turned_factor[:, rank : rank + 1]).astype(BF16)
-            scaled[place, rank * ROWS : (rank + 1) * ROWS] = rows
 
     def page_terms(place, half, tile):
         span = pl.ds(pl.multiple_of(half * HALF + tile * TILE, TILE), TILE)
@@ -240,17 +239,12 @@
     c_pg_y = copy(pg_out, pg_far, PG_Y, to_far)
     c_loss_y = copy(loss_out.at[1], loss_far, LOSS_Y, to_far)
 
-    for tile in range(HALF // TILE):
-        page_terms(ocore, oyh, tile)
-    c_pg_far.start()
     mark = lax.broadcasted_iota(jnp.int32, (8, ROWS), 1) % LQ == 0
     first, second = [jnp.sum(jnp.where(mark, each, 0.0), keepdims=True) for each in losses]
     own_loss = jnp.where(core == 0, first, second)
     sib_loss = jnp.where(core == 0, second, first)
     loss_out[0] = jnp.broadcast_to(sib_loss, (8, E))
     c_loss_sib.start()
-    for tile in range(HALF // TILE):
-        page_terms(core, oyh, tile)
 
     def backward(step, carry):
         rank = NZ - 1 - step
@@ -271,7 +265,38 @@
                 xplus(step_x),
             ).start()
 
+        return carry
+
+    lax.fori_loop(0, NZ, backward, 0, unroll=2)
+    for place in range(2):
+        columns = factors[place].T
+        for rank in range(NZ):
+            rows = q_all[zplus(offset(rank))].reshape(ROWS, E).astype(F32)
+            rows = (rows * columns[:, rank : rank + 1]).astype(BF16)
+            scaled[place, rank * ROWS : (rank + 1) * ROWS] = rows
+
+    def sum_x(step, carry):
+        rank = NZ - 1 - step
+        copy(qg_sent.at[rank, pl.ds(0, NX - 1)], in_x.at[rank], SUM_X + rank, xplus(1)).wait_recv()
+        total = qg[rank, x]
+        for slot in range(NX - 1):
+            total = total + in_x[rank, slot].astype(F32)
+        out_z[rank] = total
+
+        @pl.when(rank > 0)
+        def _():
+            copy(out_z.at[rank], in_z.at[rank], SUM_Z + rank, {"z": zplus(offset(rank))}).start()
+
+        late, near_now = step // 2 % 2, step // 4
+        page_terms(
+            late * core + (1 - late) * ocore, near_now * yh + (1 - near_now) * oyh, step % 2
+        )
+
         @pl.when(step == 1)
+        def _():
+            c_pg_far.start()
+
+        @pl.when(step == 4)
         def _():
             c_pg_far.wait_recv()
             pg_out[...] = pg_sum[core, far] + pg_sib[0]
@@ -280,27 +305,7 @@
             loss_out[1] = jnp.broadcast_to(own_loss, (8, E)) + loss_sib[...]
             c_loss_y.start()
 
-        return carry
-
-    lax.fori_loop(0, NZ, backward, 0)
-    def sum_x(step, carry):
-        rank = NZ - 1 - step
-        copy(qg_sent.at[rank, pl.ds(0, NX - 1)], in_x.at[rank], SUM_X + rank, xplus(1)).wait_recv()
-        total = qg[rank, x]
-        for slot in range(NX - 1):
-            total = total + in_x[rank, slot].astype(F32)
-        out_z[rank] = total
-
-        @pl.when(rank > 0)
-        def _():
-            copy(out_z.at[rank], in_z.at[rank], SUM_Z + rank, {"z": zplus(offset(rank))}).start()
-
-        @pl.when(step % 2 == 1)
-        def _():
-            late = step // 4
-            page_terms(late * core + (1 - late) * ocore, yh, step // 2 % 2)
-
-        @pl.when(step == 3)
+        @pl.when(step == 5)
         def _():
             c_pg_near.start()
 
@@ -345,7 +350,7 @@
 def on_device(queries, pages, pad_counts, labels):
     vmem = pl.BlockSpec(memory_space=pltpu.VMEM)
     smem = pl.BlockSpec(memory_space=pltpu.SMEM)
-    hbm = pl.BlockSpec(memory_space=pl.ANY)
+    hbm = pl.BlockSpec(memory_space=pltpu.HBM)
     scratch = [
         pltpu.VMEM((NZ, NX, 2, LQ, E), BF16),
         pltpu.VMEM((2, 2, HALF, E), BF16),
@@ -356,7 +361,7 @@
         pltpu.VMEM((8, 2 * E), F32),
         pltpu.VMEM((2, 8, ROWS), F32),
         pltpu.VMEM((2 * E, ROWS), BF16),
-        pltpu.VMEM((2, LP, ROWS), F32),
+        pltpu.VMEM((2, 2, LP, ROWS), F32),
         pltpu.VMEM((2, LP, ALL), BF16),
         pltpu.VMEM((2, NZ, ROWS), F32),
         pltpu.VMEM((2, NZ, ROWS), F32),
@@ -393,7 +398,7 @@
         out_specs=(vmem, vmem, smem),
         scratch_shapes=scratch,
         compiler_params=pltpu.CompilerParams(
-            collective_id=0, has_side_effects=True, vmem_limit_bytes=56 * 1024 * 1024
+            collective_id=0, has_side_effects=True, vmem_limit_bytes=40 * 1024 * 1024
         ),
         cost_estimate=pl.CostEstimate(
             flops=flops, bytes_accessed=2 << 20, transcendentals=ALL * 2 * LP

time: 52.5 us -> 50.4 us (0.960)
  Pallas kernels: 46.2 us -> 43.5 us
  local copies, waits for them, and re-layouts: 3.04 us -> 3.61 us
    pallas_call x1, Pallas kernels: 46.2 us -> 43.5 us  [on_device(): pl.pallas_call(kernel, out_shape=(jax.ShapeDtypeStruct(queries.shape, F32...]
    unnamed x2 -> x8, local copies, waits for them, and re-layouts: 3.04 us -> 3.61 us
where the time goes in v3:
time: 50.4 us; the launch traced here: 50.1 us
  Pallas kernels  43.5 us (86%)
  local copies, waits for them, and re-layouts  3.61 us (7%)
  between operations  3.03 us (6%)
    pallas_call x1, Pallas kernels, on_device(): pl.pallas_call(kernel, out_shape=(jax.ShapeDtypeStruct(queries.shape, F32...  43.5 us
    unnamed x8, local copies, waits for them, and re-layouts  3.61 us

profile of v3, /device:TPU:1, one launch (start us, length us, event | category | flops | bytes accessed | tf_op | source)
XLA Modules:
  0.0 50.1 jit_solution(11322873689050228570)
XLA Ops:
  1.3 0.0 copy-start.2
  1.3 0.7 %copy-done.2 = s32[256,1]{0,1:T(1,128)S(1)} copy-done((s32[256,1]{0,1:T(1,128)S(1)}, s32[256,1]{0,1:T(1,128)}, u32[]{:S(2)}) %copy-start.2) | copy-done | bytes 1048
  2.0 0.0 copy-start
  2.0 0.9 %copy-done = bf16[1,512,128]{2,1,0:T(8,128)(2,1)S(1)} copy-done((bf16[1,512,128]{2,1,0:T(8,128)(2,1)S(1)}, bf16[1,512,128]{2,1,0:T(8,128)(2,1)}, u32[]{:S(2)}) %copy-start) | copy-done | bytes 131096
  2.9 0.0 copy-start.1
  2.9 0.7 %copy-done.1 = bf16[2,32,128]{2,1,0:T(8,128)(2,1)S(1)} copy-done((bf16[2,32,128]{2,1,0:T(8,128)(2,1)S(1)}, bf16[2,32,128]{2,1,0:T(8,128)(2,1)}, u32[]{:S(2)}) %copy-start.1) | copy-done | bytes 16408
  3.6 43.5 %shard_map.67 = (f32[2,32,128]{2,1,0:T(8,128)S(1)}, f32[1,512,128]{2,1,0:T(8,128)S(1)}, f32[1]{0:T(128)}) custom-call(bf16[2,32,128]{2,1,0:T(8,128)(2,1)S(1)} %copy-done.1, bf16[1,512,128]{2,1,0:T(8,128)(2,1)S(1)} %copy-done, s32[1]{0:T(128)S(6)} %copy.10.pad_ref, s32[1,256]{1,0:T(1,128)S(1)} %bitcast.1), custom_call_target="tpu_custom_call" | custom-call | flops 3221225472 | bytes 2097152 | tf_op jit(solution)/shard_map/pallas_call | solution.py:390
  47.1 0.6 %copy.11 = f32[2,32,128]{2,1,0:T(8,128)} copy(f32[2,32,128]{2,1,0:T(8,128)S(1)} %get-tuple-element.6) | data formatting | bytes 65536
  47.7 0.7 %copy.12 = f32[1,512,128]{2,1,0:T(8,128)} copy(f32[1,512,128]{2,1,0:T(8,128)S(1)} %get-tuple-element.7) | data formatting | bytes 524288
Async XLA Ops:
  1.3 0.7 %copy-start.2 = (s32[256,1]{0,1:T(1,128)S(1)}, s32[256,1]{0,1:T(1,128)}, u32[]{:S(2)}) copy-start(s32[256,1]{0,1:T(1,128)} %param.7) | copy-start | bytes 3076
  2.0 0.9 %copy-start = (bf16[1,512,128]{2,1,0:T(8,128)(2,1)S(1)}, bf16[1,512,128]{2,1,0:T(8,128)(2,1)}, u32[]{:S(2)}) copy-start(bf16[1,512,128]{2,1,0:T(8,128)(2,1)} %page_ref.1) | copy-start | bytes 393220
  2.9 0.7 %copy-start.1 = (bf16[2,32,128]{2,1,0:T(8,128)(2,1)S(1)}, bf16[2,32,128]{2,1,0:T(8,128)(2,1)}, u32[]{:S(2)}) copy-start(bf16[2,32,128]{2,1,0:T(8,128)(2,1)} %q_ref.1) | copy-start | bytes 49156

commit v4 on v3

--- a/solution.py
+++ b/solution.py
@@ -85,6 +85,7 @@
     partners = [to_sib, to_far, to_y, to_corner]
     partners += [xplus(step) for step in range(1, NX)]
     partners += [{"z": zplus(step)} for step in range(1, NZ)]
+    partners += [{"z": zplus(step), "yl": oyl} for step in range(1, NZ)]
     for where in partners:
         pl.semaphore_signal(barrier, inc=1, device_id=where, device_id_type=MESH)
 
@@ -124,13 +125,15 @@
         return copy(block, block, TILE_X + rank, xplus(1))
 
     c_tile_y.start()
+    for rank in range(1, NZ):
+        for line_of in ({}, to_y):
+            where = {"z": zplus(NZ - offset(rank)), **line_of}
+            copy(own_tile, own_tile, TILE_Z + rank, where).start()
     for each in c_far_page:
         each.start()
     c_aux.start()
     c_sib_page.start()
     c_tile_y.wait_recv()
-    for each in c_tile_z:
-        each.start()
     send_x(0)
 
     c_aux.wait_recv()
@@ -246,6 +249,17 @@
     loss_out[0] = jnp.broadcast_to(sib_loss, (8, E))
     c_loss_sib.start()
 
+    for place in range(2):
+        columns = factors[place].T
+        for rank in range(NZ):
+            rows = q_all[zplus(offset(rank))].reshape(ROWS, E).astype(F32)
+            rows = (rows * columns[:, rank : rank + 1]).astype(BF16)
+            scaled[place, rank * ROWS : (rank + 1) * ROWS] = rows
+
+    for tile in range(HALF // TILE):
+        page_terms(ocore, oyh, tile)
+    c_pg_far.start()
+
     def backward(step, carry):
         rank = NZ - 1 - step
         lanes = pl.ds(pl.multiple_of(rank * ROWS, ROWS), ROWS)
@@ -267,14 +281,7 @@
 
         return carry
 
-    lax.fori_loop(0, NZ, backward, 0, unroll=2)
-    for place in range(2):
-        columns = factors[place].T
-        for rank in range(NZ):
-            rows = q_all[zplus(offset(rank))].reshape(ROWS, E).astype(F32)
-            rows = (rows * columns[:, rank : rank + 1]).astype(BF16)
-            scaled[place, rank * ROWS : (rank + 1) * ROWS] = rows
-
+    lax.fori_loop(0, NZ, backward, 0, unroll=4)
     def sum_x(step, carry):
         rank = NZ - 1 - step
         copy(qg_sent.at[rank, pl.ds(0, NX - 1)], in_x.at[rank], SUM_X + rank, xplus(1)).wait_recv()
@@ -287,16 +294,15 @@
         def _():
             copy(out_z.at[rank], in_z.at[rank], SUM_Z + rank, {"z": zplus(offset(rank))}).start()
 
-        late, near_now = step // 2 % 2, step // 4
-        page_terms(
-            late * core + (1 - late) * ocore, near_now * yh + (1 - near_now) * oyh, step % 2
-        )
+        @pl.when(step < 6)
+        def _():
+            piece = step + 2
+            late, near_now = piece // 2 % 2, piece // 4
+            page_terms(
+                late * core + (1 - late) * ocore, near_now * yh + (1 - near_now) * oyh, piece % 2
+            )
 
         @pl.when(step == 1)
-        def _():
-            c_pg_far.start()
-
-        @pl.when(step == 4)
         def _():
             c_pg_far.wait_recv()
             pg_out[...] = pg_sum[core, far] + pg_sib[0]
@@ -305,7 +311,7 @@
             loss_out[1] = jnp.broadcast_to(own_loss, (8, E)) + loss_sib[...]
             c_loss_y.start()
 
-        @pl.when(step == 5)
+        @pl.when(step == 3)
         def _():
             c_pg_near.start()
 

time: 50.4 us -> 47.9 us (0.950)
  the two profiles are of different devices: /device:TPU:1 before, /device:TPU:8 now
where the time goes in v4:
time: 47.9 us; the launch traced here: 47.7 us
  Pallas kernels  41.1 us (86%)
  local copies, waits for them, and re-layouts  3.61 us (8%)
  between operations  3.03 us (6%)
    pallas_call x1, Pallas kernels, on_device(): pl.pallas_call(kernel, out_shape=(jax.ShapeDtypeStruct(queries.shape, F32...  41.1 us
    unnamed x8, local copies, waits for them, and re-layouts  3.61 us

profile of v4, /device:TPU:8, one launch (start us, length us, event | category | flops | bytes accessed | tf_op | source)
XLA Modules:
  0.0 47.7 jit_solution(15615924568051339093)
XLA Ops:
  1.3 0.0 copy-start.2
  1.3 0.7 %copy-done.2 = s32[256,1]{0,1:T(1,128)S(1)} copy-done((s32[256,1]{0,1:T(1,128)S(1)}, s32[256,1]{0,1:T(1,128)}, u32[]{:S(2)}) %copy-start.2) | copy-done | bytes 1048
  2.0 0.0 copy-start
  2.0 0.9 %copy-done = bf16[1,512,128]{2,1,0:T(8,128)(2,1)S(1)} copy-done((bf16[1,512,128]{2,1,0:T(8,128)(2,1)S(1)}, bf16[1,512,128]{2,1,0:T(8,128)(2,1)}, u32[]{:S(2)}) %copy-start) | copy-done | bytes 131096
  2.9 0.0 copy-start.1
  2.9 0.7 %copy-done.1 = bf16[2,32,128]{2,1,0:T(8,128)(2,1)S(1)} copy-done((bf16[2,32,128]{2,1,0:T(8,128)(2,1)S(1)}, bf16[2,32,128]{2,1,0:T(8,128)(2,1)}, u32[]{:S(2)}) %copy-start.1) | copy-done | bytes 16408
  3.6 41.1 %shard_map.67 = (f32[2,32,128]{2,1,0:T(8,128)S(1)}, f32[1,512,128]{2,1,0:T(8,128)S(1)}, f32[1]{0:T(128)}) custom-call(bf16[2,32,128]{2,1,0:T(8,128)(2,1)S(1)} %copy-done.1, bf16[1,512,128]{2,1,0:T(8,128)(2,1)S(1)} %copy-done, s32[1]{0:T(128)S(6)} %copy.10.pad_ref, s32[1,256]{1,0:T(1,128)S(1)} %bitcast.1), custom_call_target="tpu_custom_call" | custom-call | flops 3221225472 | bytes 2097152 | tf_op jit(solution)/shard_map/pallas_call | solution.py:396
  44.7 0.6 %copy.11 = f32[2,32,128]{2,1,0:T(8,128)} copy(f32[2,32,128]{2,1,0:T(8,128)S(1)} %get-tuple-element.6) | data formatting | bytes 65536
  45.3 0.7 %copy.12 = f32[1,512,128]{2,1,0:T(8,128)} copy(f32[1,512,128]{2,1,0:T(8,128)S(1)} %get-tuple-element.7) | data formatting | bytes 524288
Async XLA Ops:
  1.3 0.7 %copy-start.2 = (s32[256,1]{0,1:T(1,128)S(1)}, s32[256,1]{0,1:T(1,128)}, u32[]{:S(2)}) copy-start(s32[256,1]{0,1:T(1,128)} %param.7) | copy-start | bytes 3076
  2.0 0.9 %copy-start = (bf16[1,512,128]{2,1,0:T(8,128)(2,1)S(1)}, bf16[1,512,128]{2,1,0:T(8,128)(2,1)}, u32[]{:S(2)}) copy-start(bf16[1,512,128]{2,1,0:T(8,128)(2,1)} %page_ref.1) | copy-start | bytes 393220
  2.9 0.7 %copy-start.1 = (bf16[2,32,128]{2,1,0:T(8,128)(2,1)S(1)}, bf16[2,32,128]{2,1,0:T(8,128)(2,1)}, u32[]{:S(2)}) copy-start(bf16[2,32,128]{2,1,0:T(8,128)(2,1)} %q_ref.1) | copy-start | bytes 49156

commit v5 on v4

--- a/solution.py
+++ b/solution.py
@@ -42,7 +42,7 @@
 
 
 def kernel(
-    q_ref, page_ref, pad_ref, label_ref,
+    in_ref, pad_ref,
     qg_ref, pg_ref, loss_ref,
     q_all, p_all, p_turned, bias, labels, aux, aux_sib, labels_wide, group_ones,
     raw, weights, tops, sums, labels_rank, scaled, factors, pg_sum,
@@ -55,9 +55,13 @@
     oyl, ocore, oyh = 1 - yl, 1 - core, 1 - yh
 
     loads = [
-        pltpu.make_async_copy(q_ref.at[yh], q_all.at[z, x, yl], load_sem.at[0]),
-        pltpu.make_async_copy(page_ref.at[0], p_all.at[core, yh], load_sem.at[1]),
-        pltpu.make_async_copy(label_ref, labels, load_sem.at[2]),
+        pltpu.make_async_copy(
+            in_ref.at[pl.ds(pl.multiple_of(HALF + yh * LQ, LQ), LQ)],
+            q_all.at[z, x, yl],
+            load_sem.at[0],
+        ),
+        pltpu.make_async_copy(in_ref.at[pl.ds(0, HALF)], p_all.at[core, yh], load_sem.at[1]),
+        pltpu.make_async_copy(in_ref.at[pl.ds(HALF + 2 * LQ, 16)], labels, load_sem.at[2]),
     ]
     for each in loads:
         each.start()
@@ -95,7 +99,9 @@
     for each in loads:
         each.wait()
     row = lax.broadcasted_iota(jnp.int32, (8, 2 * E), 0)
-    aux[...] = jnp.where(row == 0, labels[...].astype(F32), pad_ref[0].astype(F32))
+    held = labels[...].astype(F32)
+    label_row = jnp.concatenate([held[0:1], held[1:2]], axis=1)
+    aux[...] = jnp.where(row == 0, label_row, pad_ref[0].astype(F32))
     pl.semaphore_wait(barrier, len(partners))
 
     own_tile = q_all.at[z, x, yl]
@@ -117,7 +123,7 @@
 
     def send_x(rank):
         block = q_all.at[zplus(offset(rank)), x]
-        for step in range(1, NX):
+        for step in (2, 1, 3):
             copy(block, block, TILE_X + rank, xplus(step)).start()
 
     def three(rank):
@@ -125,8 +131,8 @@
         return copy(block, block, TILE_X + rank, xplus(1))
 
     c_tile_y.start()
-    for rank in range(1, NZ):
-        for line_of in ({}, to_y):
+    for rank in range(NZ - 1, 0, -1):
+        for line_of in (to_y, {}):
             where = {"z": zplus(NZ - offset(rank)), **line_of}
             copy(own_tile, own_tile, TILE_Z + rank, where).start()
     for each in c_far_page:
@@ -214,14 +220,17 @@
             labels_rank[place, rank : rank + 1] = label_rows[place]
 
     losses = []
+    parts = []
     for place in range(2):
         smooth = tops[place] * score_scale + jnp.log(sums[place])
-        high = smooth.astype(BF16)
-        rest = smooth - high.astype(F32)
-        middle = rest.astype(BF16)
-        low = (rest - middle.astype(F32)).astype(BF16)
-        ones = group_ones[...]
-        similarity = (dot(low, ones) + dot(middle, ones)) + dot(high, ones)
+        for _ in range(3):
+            part = smooth.astype(BF16).astype(F32)
+            parts.append(part)
+            smooth = smooth - part
+    summed = dot(jnp.concatenate(parts, axis=0).astype(BF16), group_ones[...])
+    for place in range(2):
+        high, middle, low = [summed[(3 * place + k) * NZ : (3 * place + k + 1) * NZ] for k in range(3)]
+        similarity = (low + middle) + high
         sign = 2.0 * labels_rank[place] - 1.0
         lean = -sign * (gain * (similarity - centre))
         small = jnp.exp(-jnp.abs(lean))
@@ -271,7 +280,7 @@
         turned = gradient.T.reshape(NX, 2, LQ, E)
         qg[rank] = turned
         qg_sent[rank] = turned.astype(BF16)
-        for step_x in range(1, NX):
+        for step_x in (2, 1, 3):
             copy(
                 qg_sent.at[rank, (x + step_x) % NX],
                 in_x.at[rank, step_x - 1],
@@ -362,7 +371,7 @@
         pltpu.VMEM((2, 2, HALF, E), BF16),
         pltpu.VMEM((2, E, LP), BF16),
         pltpu.VMEM((2, LP, E), F32),
-        pltpu.VMEM((1, 2 * E), jnp.int32),
+        pltpu.VMEM((16, E), BF16),
         pltpu.VMEM((8, 2 * E), F32),
         pltpu.VMEM((8, 2 * E), F32),
         pltpu.VMEM((2, 8, ROWS), F32),
@@ -392,6 +401,14 @@
         pltpu.SemaphoreType.DMA((COPIES,)),
         pltpu.SemaphoreType.DMA((COPIES,)),
     ]
+    taken = jnp.concatenate(
+        [
+            pages.reshape(HALF, E),
+            queries.reshape(2 * LQ, E),
+            labels.astype(BF16).reshape(2, E),
+            jnp.zeros((14, E), BF16),
+        ]
+    )
     flops = 3 * 2 * ALL * (2 * LP) * E
     return pl.pallas_call(
         kernel,
@@ -400,7 +417,7 @@
             jax.ShapeDtypeStruct(pages.shape, F32),
             jax.ShapeDtypeStruct((1,), F32),
         ),
-        in_specs=[hbm, hbm, smem, hbm],
+        in_specs=[hbm, smem],
         out_specs=(vmem, vmem, smem),
         scratch_shapes=scratch,
         compiler_params=pltpu.CompilerParams(
@@ -409,7 +426,7 @@
         cost_estimate=pl.CostEstimate(
             flops=flops, bytes_accessed=2 << 20, transcendentals=ALL * 2 * LP
         ),
-    )(queries, pages, pad_counts, labels.reshape(1, -1))
+    )(taken, pad_counts)
 
 
 def solution(mesh):

time: 47.9 us -> 47.8 us (level)
  local copies, waits for them, and re-layouts: 3.61 us -> 2.07 us
  other arithmetic: 0 us -> 1.08 us
    unnamed x8 -> x4, local copies, waits for them, and re-layouts: 3.61 us -> 1.99 us
    concatenate x0 -> x1, other arithmetic: none -> 1.06 us  [on_device(): jnp.concatenate([pages.reshape(HALF, E), queries.reshape(2 * LQ, E), labe...]
where the time goes in v5:
time: 47.8 us; the launch traced here: 47.6 us
  Pallas kernels  41.3 us (86%)
  between operations  3.12 us (7%)
  local copies, waits for them, and re-layouts  2.07 us (4%)
  other arithmetic  1.08 us (2%)
    pallas_call x1, Pallas kernels, on_device(): pl.pallas_call(kernel, out_shape=(jax.ShapeDtypeStruct(queries.shape, F32...  41.3 us
    unnamed x4, local copies, waits for them, and re-layouts  1.99 us
    concatenate x1, other arithmetic, on_device(): jnp.concatenate([pages.reshape(HALF, E), queries.reshape(2 * LQ, E), labe...  1.06 us

profile of v5, /device:TPU:8, one launch (start us, length us, event | category | flops | bytes accessed | tf_op | source)
XLA Modules:
  0.0 47.6 jit_solution(6281299046513829017)
XLA Ops:
  1.3 0.0 copy-start
  1.3 0.7 %copy-done = s32[256,1]{0,1:T(1,128)S(1)} copy-done((s32[256,1]{0,1:T(1,128)S(1)}, s32[256,1]{0,1:T(1,128)}, u32[]{:S(2)}) %copy-start) | copy-done | bytes 1048
  2.0 0.1 pad.3.clone
  2.1 1.1 %maximum_maximum_fusion.in_ref = bf16[592,128]{1,0:T(8,128)(2,1)S(1)} fusion(bf16[2,128]{1,0:T(2,128)(2,1)S(1)} %bitcast.5, bf16[64,128]{1,0:T(8,128)(2,1)} %bitcast.4, bf16[512,128]{1,0:T(8,128)(2,1)} %bitcast.3, bf16[592]{0:T(1024)(128)(2,1)S(1)} %pad.3.clone), kind=kLoop, calls=%fused_computation | loop fusion | flops 606208 | bytes 300704 | tf_op jit(solution)/shard_map/concatenate | solution.py:404
  3.1 41.3 %shard_map.67 = (f32[2,32,128]{2,1,0:T(8,128)S(1)}, f32[1,512,128]{2,1,0:T(8,128)S(1)}, f32[1]{0:T(128)}) custom-call(bf16[592,128]{1,0:T(8,128)(2,1)S(1)} %maximum_maximum_fusion.in_ref, s32[1]{0:T(128)S(6)} %copy.10.pad_ref), custom_call_target="tpu_custom_call" | custom-call | flops 3221225472 | bytes 2097152 | tf_op jit(solution)/shard_map/pallas_call | solution.py:413
  44.4 0.6 %copy.11 = f32[2,32,128]{2,1,0:T(8,128)} copy(f32[2,32,128]{2,1,0:T(8,128)S(1)} %get-tuple-element.6) | data formatting | bytes 65536
  45.0 0.7 %copy.12 = f32[1,512,128]{2,1,0:T(8,128)} copy(f32[1,512,128]{2,1,0:T(8,128)S(1)} %get-tuple-element.7) | data formatting | bytes 524288
  (2 shorter events, 0.0 us)
Async XLA Ops:
  1.3 0.7 %copy-start = (s32[256,1]{0,1:T(1,128)S(1)}, s32[256,1]{0,1:T(1,128)}, u32[]{:S(2)}) copy-start(s32[256,1]{0,1:T(1,128)} %param.7) | copy-start | bytes 3076

commit v6 on v5

--- a/solution.py
+++ b/solution.py
@@ -28,8 +28,8 @@
 TILE_Z, TILE_X = 7, 7 + NZ
 SUM_X, SUM_Z = TILE_X + NZ, TILE_X + 2 * NZ
 FINAL = SUM_Z + NZ
-PG_FAR, PG_NEAR, PG_Y, LOSS_SIB, LOSS_Y = range(FINAL + 3, FINAL + 8)
-COPIES = LOSS_Y + 1
+PG_NEAR, LOSS_SIB, LOSS_Y, PG_FAR, PG_Y = FINAL + 3, FINAL + 4, FINAL + 5, FINAL + 6, FINAL + 8
+COPIES = PG_Y + 2
 
 
 def dot(left, right, dims=((1,), (0,))):
@@ -244,11 +244,19 @@
         pg_sum[place, span] = dot(weights[place, span], scaled[place])
 
     near = pl.ds(pl.multiple_of(yh * HALF, HALF), HALF)
-    far = pl.ds(pl.multiple_of(oyh * HALF, HALF), HALF)
-    c_pg_far = copy(pg_sum.at[ocore, far], pg_sib.at[0], PG_FAR, to_sib)
+    def far_tile(tile):
+        return pl.ds(pl.multiple_of(oyh * HALF + tile * TILE, TILE), TILE)
+
+    def pg_to_sib(tile):
+        rows = pl.ds(pl.multiple_of(tile * TILE, TILE), TILE)
+        return copy(pg_sum.at[ocore, far_tile(tile)], pg_sib.at[0, rows], PG_FAR + tile, to_sib)
+
+    def pg_to_far(tile):
+        rows = pl.ds(pl.multiple_of(tile * TILE, TILE), TILE)
+        return copy(pg_out.at[rows], pg_far.at[rows], PG_Y + tile, to_far)
+
     c_pg_near = copy(pg_sum.at[ocore, near], pg_sib.at[1], PG_NEAR, to_sib)
     c_loss_sib = copy(loss_out.at[0], loss_sib, LOSS_SIB, to_sib)
-    c_pg_y = copy(pg_out, pg_far, PG_Y, to_far)
     c_loss_y = copy(loss_out.at[1], loss_far, LOSS_Y, to_far)
 
     mark = lax.broadcasted_iota(jnp.int32, (8, ROWS), 1) % LQ == 0
@@ -267,7 +275,7 @@
 
     for tile in range(HALF // TILE):
         page_terms(ocore, oyh, tile)
-    c_pg_far.start()
+        pg_to_sib(tile).start()
 
     def backward(step, carry):
         rank = NZ - 1 - step
@@ -311,11 +319,15 @@
                 late * core + (1 - late) * ocore, near_now * yh + (1 - near_now) * oyh, piece % 2
             )
 
+        @pl.when(step < 2)
+        def _():
+            rows = pl.ds(pl.multiple_of(step * TILE, TILE), TILE)
+            pg_to_sib(step).wait_recv()
+            pg_out[rows] = pg_sum[core, far_tile(step)] + pg_sib[0, rows]
+            pg_to_far(step).start()
+
         @pl.when(step == 1)
         def _():
-            c_pg_far.wait_recv()
-            pg_out[...] = pg_sum[core, far] + pg_sib[0]
-            c_pg_y.start()
             c_loss_sib.wait_recv()
             loss_out[1] = jnp.broadcast_to(own_loss, (8, E)) + loss_sib[...]
             c_loss_y.start()
@@ -348,11 +360,13 @@
     c_fin[2].wait_recv()
     c_fin[0].wait_recv()
     qg_ref[oyh] = in_fin[2] + in_fin[1]
-    c_pg_y.wait_recv()
+    for tile in range(HALF // TILE):
+        pg_to_far(tile).wait_recv()
     pg_ref[0] = (near_sum + pg_far[...]) * score_scale
 
     sent = [c_tile_y, *c_far_page, *c_sib_far, c_sib_page, c_aux, *c_tile_z, *c_fin]
-    sent += [c_pg_far, c_pg_near, c_loss_sib, c_pg_y, c_loss_y]
+    sent += [c_pg_near, c_loss_sib, c_loss_y]
+    sent += [each(tile) for each in (pg_to_sib, pg_to_far) for tile in range(HALF // TILE)]
     for each in sent:
         each.wait_send()
     for rank in range(NZ):

time: 47.8 us -> 47.9 us (level)
  no operation moved by 1% of the time
where the time goes in v6:
time: 47.9 us; the launch traced here: 47.7 us
  Pallas kernels  41.4 us (86%)
  between operations  3.12 us (7%)
  local copies, waits for them, and re-layouts  2.07 us (4%)
  other arithmetic  1.08 us (2%)
    pallas_call x1, Pallas kernels, on_device(): pl.pallas_call(kernel, out_shape=(jax.ShapeDtypeStruct(queries.shape, F32...  41.4 us
    unnamed x4, local copies, waits for them, and re-layouts  1.99 us
    concatenate x1, other arithmetic, on_device(): jnp.concatenate([pages.reshape(HALF, E), queries.reshape(2 * LQ, E), labe...  1.06 us

profile of v6, /device:TPU:8, one launch (start us, length us, event | category | flops | bytes accessed | tf_op | source)
XLA Modules:
  0.0 47.7 jit_solution(18264632491007711343)
XLA Ops:
  1.3 0.0 copy-start
  1.3 0.7 %copy-done = s32[256,1]{0,1:T(1,128)S(1)} copy-done((s32[256,1]{0,1:T(1,128)S(1)}, s32[256,1]{0,1:T(1,128)}, u32[]{:S(2)}) %copy-start) | copy-done | bytes 1048
  2.0 0.1 pad.3.clone
  2.1 1.1 %maximum_maximum_fusion.in_ref = bf16[592,128]{1,0:T(8,128)(2,1)S(1)} fusion(bf16[2,128]{1,0:T(2,128)(2,1)S(1)} %bitcast.5, bf16[64,128]{1,0:T(8,128)(2,1)} %bitcast.4, bf16[512,128]{1,0:T(8,128)(2,1)} %bitcast.3, bf16[592]{0:T(1024)(128)(2,1)S(1)} %pad.3.clone), kind=kLoop, calls=%fused_computation | loop fusion | flops 606208 | bytes 300704 | tf_op jit(solution)/shard_map/concatenate | solution.py:418
  3.1 41.4 %shard_map.67 = (f32[2,32,128]{2,1,0:T(8,128)S(1)}, f32[1,512,128]{2,1,0:T(8,128)S(1)}, f32[1]{0:T(128)}) custom-call(bf16[592,128]{1,0:T(8,128)(2,1)S(1)} %maximum_maximum_fusion.in_ref, s32[1]{0:T(128)S(6)} %copy.10.pad_ref), custom_call_target="tpu_custom_call" | custom-call | flops 3221225472 | bytes 2097152 | tf_op jit(solution)/shard_map/pallas_call | solution.py:427
  44.6 0.6 %copy.11 = f32[2,32,128]{2,1,0:T(8,128)} copy(f32[2,32,128]{2,1,0:T(8,128)S(1)} %get-tuple-element.6) | data formatting | bytes 65536
  45.2 0.7 %copy.12 = f32[1,512,128]{2,1,0:T(8,128)} copy(f32[1,512,128]{2,1,0:T(8,128)S(1)} %get-tuple-element.7) | data formatting | bytes 524288
  (2 shorter events, 0.0 us)
Async XLA Ops:
  1.3 0.7 %copy-start = (s32[256,1]{0,1:T(1,128)S(1)}, s32[256,1]{0,1:T(1,128)}, u32[]{:S(2)}) copy-start(s32[256,1]{0,1:T(1,128)} %param.7) | copy-start | bytes 3076
